TPU v7x, 32 devices: a whole 2x2x4 slice. The times are simulated.
32 devices in a mesh: light: 8 (over y, x, core), tile: 4 (over z).
Axes of the slice: x: 2, y: 2, z: 4, core: 2. Of those that a mesh axis runs over, the one named last changes fastest.
Arguments:
- density: float32 [128, 32, 2048], P('light', 'tile'), may hold values from 0.03 to 9, as said below
- bin_index: int32 [128, 32, 2048], P('light', 'tile'), may hold values from 0 to 127
- transfer: float32 [4, 128], replicated, may hold values from 0.1 to 1
- depth_order: int32 [4], replicated, may hold values from 0 to 3, each once
Outputs:
- picture: float32 [4, 128, 2048], P(None, 'light', 'tile')
Inputs may be any that keep to these rules, and one draw needn't show every extreme that they name: Positive density. `depth_order`: each rank of 0 to 3 once.
All inputs are finite; a program needn't handle non-finite values.
Results may differ from a plain program's by a relative error of at most 0.0003.
Values sent between devices are 32-bit elements; how exact they have to be, the bound alone decides.
No kernel may reach another device: no remote copies, remote signals or barrier semaphores. Data moves between devices by JAX's collectives and lax.ppermute only.
A program may use at most 256 MiB of HBM per device.

v0:
```python
import jax
import jax.numpy as jnp
from jax import lax
from jax.sharding import PartitionSpec as P

AMBIENT = 0.25


def padded_2(cells, sides, width):
    for axis, dim in sides:
        count = lax.axis_size(axis)
        ends = count - 1
        head = lax.slice_in_dim(cells, 0, width, axis=dim)
        tail = lax.slice_in_dim(cells, cells.shape[dim] - width, cells.shape[dim], axis=dim)
        cells = jnp.concatenate(
            [
                lax.ppermute(tail, axis, [(i, (i + 1) % count) for i in range(ends)]),
                cells,
                lax.ppermute(head, axis, [((i + 1) % count, i) for i in range(ends)]),
            ],
            axis=dim,
        )
    return cells


def entering(value, axis, join, neutral):
    count, mine = (lax.axis_size(axis), lax.axis_index(axis))
    pieces = lax.all_gather(value, axis)
    subtotal = jnp.full_like(value, 0) + jnp.asarray(neutral, value.dtype)

    def turn(position, subtotal):
        longer = join(subtotal, pieces[position])
        return jnp.where(position < mine, longer, subtotal)

    return lax.fori_loop(0, count - 1, turn, subtotal)


def add_planes(earlier, later):
    return earlier + later


def per_device(density, bin_index, transfer, depth_order):
    light_cells, depth_cells, columns = density.shape
    light_count = lax.axis_size("light")
    tile_count = lax.axis_size("tile")
    light_step = 3.0 / (light_cells * light_count)
    view_step = 3.0 / (depth_cells * tile_count)
    padded = padded_2(density, (("light", 0),), 1)
    grad_light = 0.5 * (padded[2:] - padded[:-2])
    widened = jnp.pad(density, ((0, 0), (0, 0), (1, 1)))
    grad_col = 0.5 * (widened[:, :, 2:] - widened[:, :, :-2])
    shading = 1.0 + 0.5 * jnp.tanh(grad_light + grad_col)
    looked = jnp.take(transfer, bin_index, axis=1)
    extinction = looked[3] * density
    running = jnp.cumsum(extinction, axis=0)
    slab_total = running[-1]
    upstream = entering(slab_total, "light", add_planes, jnp.zeros_like(slab_total))
    light_depth = (upstream[None] + running - extinction) * light_step
    lighting = AMBIENT + jnp.exp(-light_depth) * shading
    view_depth = extinction * view_step
    ahead_depth = jnp.cumsum(view_depth, axis=1) - view_depth
    weight = jnp.exp(-ahead_depth) * (1.0 - jnp.exp(-view_depth))
    shaded = weight * lighting
    emitted = jnp.sum(shaded[None] * looked[:3], axis=2)
    clearance = jnp.exp(-jnp.sum(view_depth, axis=1))
    partial_value = jnp.concatenate([emitted, clearance[None]], axis=0)
    pieces = lax.all_to_all(
        partial_value[:, :, None, :], "tile", split_axis=3, concat_axis=2, tiled=True
    )
    clear_all = pieces[3]
    in_front = depth_order[None, :] < depth_order[:, None]
    factors = jnp.where(in_front[None, :, :, None], clear_all[:, None, :, :], 1.0)
    ahead_clear = jnp.prod(factors, axis=2)
    colour_sum = jnp.sum(pieces[:3] * ahead_clear[None], axis=2)
    opacity = 1.0 - jnp.prod(clear_all, axis=1)
    return jnp.concatenate([colour_sum, opacity[None]], axis=0)


def solution(mesh):
    in_specs = (P("light", "tile", None), P("light", "tile", None), P(), P())
    out_specs = P(None, "light", "tile")
    return jax.shard_map(
        per_device, mesh=mesh, in_specs=in_specs, out_specs=out_specs, check_vma=False
    )
```

profile of v0, /device:TPU:0, one launch (start us, length us, event | category | flops | bytes accessed | tf_op | source)
XLA Modules:
  0.0 1023.5 jit_solution(1550186706167068103)
XLA Ops:
  0.0 0.9 fusion.16
  0.9 1.3 collective-permute-start
  2.2 3.0 collective-permute-start.1
  5.2 1.4 fusion.12
  6.6 1.5 compare_and_fusion
  8.2 0.2 copy.29
  8.4 0.1 broadcast_clamp_fusion
  8.6 860.0 %gather_fusion = f32[262144,4]{1,0:T(8,128)} fusion(f32[4,128]{0,1:T(8,128)S(1)} %copy.21, s32[262144]{0:T(1024)S(1)} %broadcast_clamp_fusion), kind=kCustom, calls=%fused_computation | custom fusion | bytes 9437184 | tf_op jit(solution)/shard_map/jit(_take)/gather | solution.py:53
  868.6 77.5 %copy.28 = f32[16,8,2048,4]{2,1,0,3:T(8,128)} copy(f32[16,8,2048,4]{3,2,1,0:T(8,128)} %bitcast) | data formatting | bytes 8388608 | tf_op jit(solution)/shard_map/jit(_take)/gather | solution.py:53
  946.1 3.0 select_bitcast_fusion
  949.1 1.9 copy-done
  951.0 0.5 fusion.14
  951.6 12.1 %all_gather.3 = f32[8,8,2048]{2,1,0:T(8,128)S(1)} all-gather(f32[1,8,2048]{2,1,0:T(8,128)S(1)} %slice.55), channel_id=1, replica_groups=mesh['light'=8,'tile'=4] {'light'}, dimensions={0}, use_global_device_ids=true | all-gather | bytes 589824 | tf_op jit(solution)/shard_map/all_gather | solution.py:28
  963.7 0.3 while.14
  964.0 1.3 broadcast_multiply_fusion
  965.3 5.2 reduce_window_sum.22
  970.5 2.9 fusion.9
  973.4 1.2 fusion
  974.7 3.1 copy.23
  977.8 3.7 bitcast_bitcast_fusion
  981.5 5.8 reshape.81
  987.2 4.9 all-to-all-start
  992.2 14.9 %all-to-all-done = f32[4,1,32768]{2,1,0:T(1,128)S(1)} async-done(((f32[4,1,32768]{2,1,0:T(1,128)}), f32[4,1,32768]{2,1,0:T(1,128)S(1)}, u32[]{:S(2)}, u32[]{:S(2)}) %all-to-all-start) | async-done | bytes 524320 | tf_op jit(solution)/shard_map/all_to_all | solution.py:67
  1007.1 0.5 broadcast.67
  1007.6 2.1 reduce
  1009.8 4.9 reshape.82
  1014.7 2.8 slice.58
  1017.5 0.3 copy.24
  1017.9 0.3 copy.25
  1018.2 4.2 multiply_reduce_fusion
  1022.4 0.3 copy.26
  1022.9 0.7 pad_maximum_fusion.3
  (28 shorter events, 0.7 us)
Async XLA Ops:
  0.0 8.5 copy-start.3
  0.9 969.6 %collective-permute-start = (f32[1,8,2048]{2,1,0:T(8,128)S(1)}, f32[1,8,2048]{2,1,0:T(8,128)S(1)}, u32[]{:S(2)}, u32[]{:S(2)}) collective-permute-start(f32[1,8,2048]{2,1,0:T(8,128)S(1)} %get-tuple-element.110), channel_id=1, source_target_pairs={{4,0},{8,4},{12,8},{16,12},{20,16},{24,20},{28,24},{5,1},{9,5},{13... | collective-permute-start | bytes 196616 | tf_op jit(solution)/shard_map/ppermute | solution.py:19
  2.2 968.3 %collective-permute-start.1 = (f32[1,8,2048]{2,1,0:T(8,128)S(1)}, f32[1,8,2048]{2,1,0:T(8,128)S(1)}, u32[]{:S(2)}, u32[]{:S(2)}) collective-permute-start(f32[1,8,2048]{2,1,0:T(8,128)S(1)} %get-tuple-element.111), channel_id=1, source_target_pairs={{0,4},{4,8},{8,12},{12,16},{16,20},{20,24},{24,28},{1,5},{5,9},{9,... | collective-permute-start | bytes 196616 | tf_op jit(solution)/shard_map/ppermute | solution.py:17
  946.1 4.9 copy-start.2
  949.1 1.9 copy-start
  970.5 2.9 copy-start.1
  981.5 10.6 %copy-start.4 = (s32[4]{0:T(128)S(1)}, s32[4]{0:T(128)}, u32[]{:S(2)}) copy-start(s32[4]{0:T(128)} %param.9) | copy-start | bytes 52
  987.2 19.9 %all-to-all-start = ((f32[4,1,32768]{2,1,0:T(1,128)}), f32[4,1,32768]{2,1,0:T(1,128)S(1)}, u32[]{:S(2)}, u32[]{:S(2)}) async-start(f32[4,1,32768]{2,1,0:T(1,128)} %reshape.81), calls=%async_computation | async-start | bytes 1048576 | tf_op jit(solution)/shard_map/all_to_all | solution.py:67
where the time goes:
time: 1030 us; the launch traced here: 1020 us
  local copies, waits for them, and re-layouts  962 us (93%)
  other arithmetic  24.6 us (2%)
  waiting for transfers between devices  14.9 us (1%)
  blocking collectives  12.1 us (1%)
    gather x2, local copies, waits for them, and re-layouts, per_device(): looked = jnp.take(transfer, bin_index, axis=1)  937 us
  transfers between devices with their start and end apart: 3, of which 1 were waited for; matrix products, arithmetic and copies ran while one was open for 93% of the time, Pallas kernels for 0%

commit v1 on v0

v1 whole, which is shorter than its diff:
```python
import functools

import jax
import jax.numpy as jnp
from jax import lax
from jax.experimental import pallas as pl
from jax.experimental.pallas import tpu as pltpu
from jax.sharding import PartitionSpec as P

AMBIENT = 0.25
LANES = 128
VMEM = pltpu.VMEM
PARAMS = pltpu.CompilerParams(vmem_limit_bytes=48 * 2**20)


def full(memory_space=VMEM):
    return pl.BlockSpec(memory_space=memory_space)


def table_rows(table_ref, channel):
    entries = table_ref.shape[1]
    return [
        jnp.broadcast_to(table_ref[channel : channel + 1, first : first + LANES], (8, LANES))
        for first in range(0, entries, LANES)
    ]


def look_up(rows, index):
    low = index if len(rows) == 1 else index & (LANES - 1)
    value = jnp.take_along_axis(rows[0], low, axis=1)
    for part in range(1, len(rows)):
        value = jnp.where(index >= part * LANES, jnp.take_along_axis(rows[part], low, axis=1), value)
    return value


def extinction_kernel(density_ref, bin_ref, table_ref, ext_ref, before_ref, total_ref):
    light_cells, _, columns = density_ref.shape
    rows = table_rows(table_ref, 3)
    for first in range(0, columns, LANES):
        at = slice(first, first + LANES)
        running = jnp.zeros((8, LANES), jnp.float32)
        for i in range(light_cells):
            ext = look_up(rows, bin_ref[i, :, at]) * density_ref[i, :, at]
            ext_ref[first // LANES, 8 * i : 8 * i + 8] = ext
            before_ref[i, :, at] = running
            running = running + ext
        total_ref[:, at] = running


def local_kernel(
    light_step, view_step, ends_ref, density_ref, bin_ref, table_ref, ext_ref, before_ref, prev_ref, next_ref,
    lit_ref, ambient_ref, clear_ref, shade_ref, entry_ref,
):
    light_cells, depth_cells, columns = density_ref.shape
    lane = lax.broadcasted_iota(jnp.int32, (8, columns), 1)
    has_prev = ends_ref[0]
    has_next = ends_ref[1]

    def shade(i, above, below):
        cells = density_ref[i]
        right = jnp.where(lane == columns - 1, 0.0, pltpu.roll(cells, columns - 1, 1))
        left = jnp.where(lane == 0, 0.0, pltpu.roll(cells, 1, 1))
        slope = 0.5 * ((below - above) + (right - left))
        shading = 1.0 + 0.5 * jnp.tanh(slope)
        faded = jnp.exp(before_ref[i] * (-light_step)) * shading
        rows = pl.ds(pl.multiple_of(i * 8, 8), 8)
        for first in range(0, columns, LANES):
            at = slice(first, first + LANES)
            shade_ref[first // LANES, rows] = faded[:, at]
            entry_ref[first // LANES, rows] = bin_ref[i, :, at]

    shade(0, jnp.where(has_prev > 0, prev_ref[...], 0.0), density_ref[1])
    shade(
        light_cells - 1,
        density_ref[light_cells - 2],
        jnp.where(has_next > 0, next_ref[...], 0.0),
    )

    @pl.loop(1, light_cells - 1)
    def _(i):
        shade(i, density_ref[i - 1], density_ref[i + 1])

    tables = [table_rows(table_ref, c) for c in range(3)]

    @pl.loop(0, columns // LANES)
    def _(tile):
        at = pl.ds(pl.multiple_of(tile * LANES, LANES), LANES)
        for half in range(0, light_cells, 8):
            clear = jnp.ones((8, LANES), jnp.float32)
            ambient = [jnp.zeros((8, LANES), jnp.float32) for _ in range(3)]
            for j in range(depth_cells):
                cells = pl.ds(half * depth_cells + j, 8, stride=depth_cells)
                further = clear * jnp.exp(ext_ref[tile, cells] * (-view_step))
                weight = clear - further
                clear = further
                lit = weight * shade_ref[tile, cells]
                index = entry_ref[tile, cells]
                for c in range(3):
                    colour = look_up(tables[c], index)
                    lit_ref[c, j, half : half + 8, at] = lit * colour
                    ambient[c] = ambient[c] + weight * colour
            for c in range(3):
                ambient_ref[c, half : half + 8, at] = AMBIENT * ambient[c]
            clear_ref[half : half + 8, at] = clear


def picture_kernel(light_step, mine_ref, upstream_ref, lit_ref, ambient_ref, clear_ref, *refs):
    *out_refs, fade_ref = refs
    _, depth_cells, light_cells, columns = lit_ref.shape
    tiles = len(out_refs)
    share = columns // tiles
    fade_ref[...] = jnp.exp(upstream_ref[...] * (-light_step))
    for step, out_ref in enumerate(out_refs):
        owner = lax.rem(mine_ref[0] + step, tiles)
        for first in range(0, share, LANES):
            at = pl.ds(pl.multiple_of(owner * share + first, LANES), LANES)
            to = slice(first, first + LANES)
            for half in range(0, light_cells, 8):
                rows = slice(half, half + 8)
                sums = [ambient_ref[c, rows, at] for c in range(3)]
                for j in range(depth_cells):
                    fade = jnp.broadcast_to(fade_ref[j : j + 1, at], (8, LANES))
                    for c in range(3):
                        sums[c] = sums[c] + fade * lit_ref[c, j, rows, at]
                for c in range(3):
                    out_ref[c, rows, to] = sums[c]
                out_ref[3, rows, to] = clear_ref[rows, at]


def combine_kernel(mine_ref, order_ref, *refs):
    *in_refs, out_ref = refs
    tiles = len(in_refs)
    rank = [order_ref[lax.rem(mine_ref[0] - step + tiles, tiles)] for step in range(tiles)]
    clear = [ref[3] for ref in in_refs]
    colour = jnp.zeros(out_ref.shape[1:], jnp.float32)
    colour = [colour, colour, colour]
    through = jnp.ones_like(colour[0])
    for step in range(tiles):
        ahead = jnp.ones_like(through)
        for other in range(tiles):
            if other != step:
                ahead = ahead * jnp.where(rank[other] < rank[step], clear[other], 1.0)
        for c in range(3):
            colour[c] = colour[c] + ahead * in_refs[step][c]
        through = through * clear[step]
    for c in range(3):
        out_ref[c] = colour[c]
    out_ref[3] = 1.0 - through


def shape(*dims):
    return jax.ShapeDtypeStruct(dims, jnp.float32)


def per_device(density, bin_index, transfer, depth_order):
    light_cells, depth_cells, columns = density.shape
    light_count = lax.axis_size("light")
    tile_count = lax.axis_size("tile")
    light_mine = lax.axis_index("light")
    tile_mine = lax.axis_index("tile").astype(jnp.int32).reshape(1)
    light_step = 3.0 / (light_cells * light_count)
    view_step = 3.0 / (depth_cells * tile_count)
    share = columns // tile_count
    tiled = (columns // LANES, light_cells * depth_cells, LANES)

    ups = [(i, i + 1) for i in range(light_count - 1)]
    prev = lax.ppermute(density[-1], "light", ups)
    nxt = lax.ppermute(density[0], "light", [(b, a) for a, b in ups])

    ext, before, total = pl.pallas_call(
        extinction_kernel,
        out_shape=[shape(*tiled), shape(*density.shape), shape(depth_cells, columns)],
        in_specs=[full()] * 3,
        out_specs=[full()] * 3,
        compiler_params=PARAMS,
        name="extinction",
    )(density, bin_index, transfer)

    upstream = jnp.zeros_like(total)
    group = total
    step = 1
    while step < light_count:
        got = lax.ppermute(group, "light", [(i, i ^ step) for i in range(light_count)])
        upstream = upstream + jnp.where((light_mine & step) > 0, got, 0.0)
        group = group + got
        step *= 2

    ends = jnp.stack([light_mine > 0, light_mine < light_count - 1]).astype(jnp.int32)
    smem = full(pltpu.SMEM)
    lit, ambient, clear = pl.pallas_call(
        functools.partial(local_kernel, light_step, view_step),
        out_shape=[
            shape(3, depth_cells, light_cells, columns),
            shape(3, light_cells, columns),
            shape(light_cells, columns),
        ],
        in_specs=[smem] + [full()] * 7,
        out_specs=[full()] * 3,
        scratch_shapes=[pltpu.VMEM(tiled, jnp.float32), pltpu.VMEM(tiled, jnp.int32)],
        compiler_params=PARAMS,
        name="local",
    )(ends, density, bin_index, transfer, ext, before, prev, nxt)

    pieces = pl.pallas_call(
        functools.partial(picture_kernel, light_step),
        out_shape=[shape(4, light_cells, share)] * tile_count,
        in_specs=[smem] + [full()] * 4,
        out_specs=[full()] * tile_count,
        scratch_shapes=[pltpu.VMEM((depth_cells, columns), jnp.float32)],
        compiler_params=PARAMS,
        name="picture",
    )(tile_mine, upstream, lit, ambient, clear)

    held = [pieces[0]]
    for step in range(1, tile_count):
        held.append(
            lax.ppermute(pieces[step], "tile", [(i, (i + step) % tile_count) for i in range(tile_count)])
        )
    return pl.pallas_call(
        combine_kernel,
        out_shape=shape(4, light_cells, share),
        in_specs=[smem, smem] + [full()] * tile_count,
        out_specs=full(),
        compiler_params=PARAMS,
        name="combine",
    )(tile_mine, depth_order, *held)


def solution(mesh):
    in_specs = (P("light", "tile", None), P("light", "tile", None), P(), P())
    out_specs = P(None, "light", "tile")
    return jax.shard_map(
        per_device, mesh=mesh, in_specs=in_specs, out_specs=out_specs, check_vma=False
    )
```

time: 1030 us -> 42.9 us (0.04)
  the two profiles are of different devices: /device:TPU:0 before, /device:TPU:9 now
where the time goes in v1:
time: 42.9 us; the launch traced here: 42.6 us
  starting transfers between devices  12.6 us (29%)
  waiting for transfers between devices  11.9 us (28%)
  Pallas kernels  9.31 us (22%)
  local copies, waits for them, and re-layouts  8.54 us (20%)
    ppermute x3, waiting for transfers between devices, per_device(): lax.ppermute(pieces[step], 'tile', [(i, (i + step) % tile_count) for i in...  11 us
    unnamed x20, local copies, waits for them, and re-layouts  7.91 us
    pallas_call x1, Pallas kernels, per_device(): pl.pallas_call(functools.partial(local_kernel, light_step, view_step), ou...  6.75 us
    ppermute x3, starting transfers between devices, per_device(): lax.ppermute(pieces[step], 'tile', [(i, (i + step) % tile_count) for i in...  3.83 us
    ppermute x3, starting transfers between devices, per_device(): lax.ppermute(group, 'light', [(i, i ^ step) for i in range(light_count)])  3.26 us
    ppermute x1, starting transfers between devices, per_device(): prev = lax.ppermute(density[-1], 'light', ups)  3.02 us
    ppermute x1, starting transfers between devices, per_device(): nxt = lax.ppermute(density[0], 'light', [(b, a) for a, b in ups])  2.53 us
    pallas_call x1, Pallas kernels, per_device(): pl.pallas_call(combine_kernel, out_shape=shape(4, light_cells, share), in...  1.27 us
  transfers between devices with their start and end apart: 8, of which 4 were waited for; matrix products, arithmetic and copies ran while one was open for 2% of the time, Pallas kernels for 16%

profile of v1, /device:TPU:9, one launch (start us, length us, event | category | flops | bytes accessed | tf_op | source)
XLA Modules:
  0.0 42.6 jit_solution(8396311168119419866)
XLA Ops:
  0.0 1.2 %copy-done = f32[16,8,2048]{2,1,0:T(8,128)S(1)} copy-done((f32[16,8,2048]{2,1,0:T(8,128)S(1)}, f32[16,8,2048]{2,1,0:T(8,128)}, u32[]{:S(2)}) %copy-start) | copy-done | bytes 1048600
  1.2 1.2 %copy-done.2 = s32[16,8,2048]{2,1,0:T(8,128)S(1)} copy-done((s32[16,8,2048]{2,1,0:T(8,128)S(1)}, s32[16,8,2048]{2,1,0:T(8,128)}, u32[]{:S(2)}) %copy-start.2) | copy-done | bytes 1048600
  2.5 0.7 %copy-done.7 = f32[4,128]{1,0:T(4,128)S(1)} copy-done((f32[4,128]{1,0:T(4,128)S(1)}, f32[4,128]{1,0:T(4,128)}, u32[]{:S(2)}) %copy-start.7) | copy-done | bytes 2072
  3.1 0.8 %extinction.1 = (f32[16,128,128]{2,1,0:T(8,128)S(1)}, f32[16,8,2048]{2,1,0:T(8,128)S(1)}, f32[8,2048]{1,0:T(8,128)S(1)}) custom-call(f32[16,8,2048]{2,1,0:T(8,128)S(1)} %copy-done, s32[16,8,2048]{2,1,0:T(8,128)S(1)} %copy-done.2, f32[4,128]{1,0:T(4,128)S(1)} %copy-done.7), custom_call_target="tpu_custom_call" | custom-call | tf_op jit(solution)/shard_map/extinction/pallas_call | solution.py:170
  3.9 0.0 copy-start.5
  3.9 1.0 %copy-done.5 = f32[16,8,2048]{2,1,0:T(8,128)} copy-done((f32[16,8,2048]{2,1,0:T(8,128)}, f32[16,8,2048]{2,1,0:T(8,128)S(1)}, u32[]{:S(2)}) %copy-start.5) | copy-done | bytes 1048600
  4.9 0.7 %collective-permute-start = (f32[8,2048]{1,0:T(8,128)S(1)}, f32[8,2048]{1,0:T(8,128)S(1)}, u32[]{:S(2)}, u32[]{:S(2)}) collective-permute-start(f32[8,2048]{1,0:T(8,128)S(1)} %get-tuple-element.15), channel_id=1, source_target_pairs={{0,4},{4,0},{8,12},{12,8},{16,20},{20,16},{24,28},{28,24},{1,5},{5... | collective-permute-start | bytes 196616 | tf_op jit(solution)/shard_map/ppermute | solution.py:183
  5.6 0.9 %collective-permute-done = f32[8,2048]{1,0:T(8,128)S(1)} collective-permute-done((f32[8,2048]{1,0:T(8,128)S(1)}, f32[8,2048]{1,0:T(8,128)S(1)}, u32[]{:S(2)}, u32[]{:S(2)}) %collective-permute-start) | collective-permute-done | bytes 65568 | tf_op jit(solution)/shard_map/ppermute | solution.py:183
  6.5 1.3 %collective-permute-start.1 = (f32[8,2048]{1,0:T(8,128)S(1)}, f32[8,2048]{1,0:T(8,128)S(1)}, u32[]{:S(2)}, u32[]{:S(2)}) collective-permute-start(f32[8,2048]{1,0:T(8,128)S(1)} %add.12), channel_id=1, source_target_pairs={{0,8},{4,12},{8,0},{12,4},{16,24},{20,28},{24,16},{28,20},{1,9},{5... | collective-permute-start | bytes 196616 | tf_op jit(solution)/shard_map/ppermute | solution.py:183
  7.8 0.6 %slice_bitcast_fusion = (f32[8,2048]{1,0:T(8,128)}, f32[8,2048]{1,0:T(8,128)S(1)}) fusion(f32[16,8,2048]{2,1,0:T(8,128)S(1)} %copy-done), kind=kLoop, calls=%fused_computation | loop fusion | bytes 262144 | tf_op jit(solution)/shard_map/squeeze | solution.py:168
  8.4 2.5 %collective-permute-start.4 = (f32[8,2048]{1,0:T(8,128)}, f32[8,2048]{1,0:T(8,128)S(1)}, u32[]{:S(2)}, u32[]{:S(2)}) collective-permute-start(f32[8,2048]{1,0:T(8,128)} %get-tuple-element.25), channel_id=1, source_target_pairs={{4,0},{8,4},{12,8},{16,12},{20,16},{24,20},{28,24},{5,1},{9,5},{13... | collective-permute-start | bytes 196616 | tf_op jit(solution)/shard_map/ppermute | solution.py:168
  11.0 3.0 %collective-permute-start.3 = (f32[8,2048]{1,0:T(8,128)S(1)}, f32[8,2048]{1,0:T(8,128)S(1)}, u32[]{:S(2)}, u32[]{:S(2)}) collective-permute-start(f32[8,2048]{1,0:T(8,128)S(1)} %get-tuple-element.26), channel_id=1, source_target_pairs={{0,4},{4,8},{8,12},{12,16},{16,20},{20,24},{24,28},{1,5},{5,9},{9,... | collective-permute-start | bytes 196616 | tf_op jit(solution)/shard_map/ppermute | solution.py:167
  14.0 0.0 collective-permute-done.1
  14.0 1.3 %collective-permute-start.2 = (f32[8,2048]{1,0:T(8,128)S(1)}, f32[8,2048]{1,0:T(8,128)S(1)}, u32[]{:S(2)}, u32[]{:S(2)}) collective-permute-start(f32[8,2048]{1,0:T(8,128)S(1)} %add.14), channel_id=1, source_target_pairs={{0,16},{4,20},{8,24},{12,28},{16,0},{20,4},{24,8},{28,12},{1,17},{... | collective-permute-start | bytes 196616 | tf_op jit(solution)/shard_map/ppermute | solution.py:183
  15.3 0.1 add_convert_fusion.ends_ref
  15.4 0.0 collective-permute-done.4.next_ref
  15.4 0.0 collective-permute-done.3.prev_ref
  15.4 0.0 copy-done.1
  15.4 1.2 %copy-done.6 = f32[16,8,2048]{2,1,0:T(8,128)S(1)} copy-done((f32[16,8,2048]{2,1,0:T(8,128)S(1)}, f32[16,8,2048]{2,1,0:T(8,128)}, u32[]{:S(2)}) %copy-start.6) | copy-done | bytes 1048600
  16.7 0.7 %copy-done.8 = f32[4,128]{1,0:T(4,128)S(1)} copy-done((f32[4,128]{1,0:T(4,128)S(1)}, f32[4,128]{1,0:T(4,128)}, u32[]{:S(2)}) %copy-start.8) | copy-done | bytes 2072
  17.3 6.7 %local.1 = (f32[3,8,16,2048]{3,2,1,0:T(8,128)}, f32[3,16,2048]{2,1,0:T(8,128)S(1)}, f32[16,2048]{1,0:T(8,128)S(1)}) custom-call(s32[2]{0:T(128)S(1)} %add_convert_fusion.ends_ref, f32[16,8,2048]{2,1,0:T(8,128)S(1)} %copy-done.1, s32[16,8,2048]{2,1,0:T(8,128)S(1)} %copy-done.3, f32[4,128]{1,0:T(4,128)S(1)} %copy-done.8, ...), custom_call_target="tpu_custom_call" | custom-call | tf_op jit(solution)/shard_map/local/pallas_call | solution.py:190
  24.1 0.0 collective-permute-done.2
  24.1 1.9 %copy-done.4 = f32[3,8,16,2048]{3,2,1,0:T(8,128)S(1)} copy-done((f32[3,8,16,2048]{3,2,1,0:T(8,128)S(1)}, f32[3,8,16,2048]{3,2,1,0:T(8,128)}, u32[]{:S(2)}) %copy-start.4) | copy-done | bytes 3145752
  26.0 0.5 %picture.1 = (f32[4,16,512]{2,1,0:T(8,128)S(1)}, f32[4,16,512]{2,1,0:T(8,128)S(1)}, f32[4,16,512]{2,1,0:T(8,128)S(1)}, f32[4,16,512]{2,1,0:T(8,128)S(1)}) custom-call(s32[1]{0:T(128)} %bitcast.mine_ref, f32[8,2048]{1,0:T(8,128)S(1)} %select_add_fusion.upstream_ref, f32[3,8,16,2048]{3,2,1,0:T(8,128)S(1)} %copy-done.4, ...), custom_call_target="tpu_custom_call" | custom-call | tf_op jit(solution)/shard_map/picture/pallas_call | solution.py:204
  26.5 1.4 %collective-permute-start.5 = (f32[4,16,512]{2,1,0:T(8,128)S(1)}, f32[4,16,512]{2,1,0:T(8,128)S(1)}, u32[]{:S(2)}, u32[]{:S(2)}) collective-permute-start(f32[4,16,512]{2,1,0:T(8,128)S(1)} %get-tuple-element.22), channel_id=1, source_target_pairs={{0,1},{1,2},{2,3},{3,0},{4,5},{5,6},{6,7},{7,4},{8,9},{9,10},{10,1... | collective-permute-start | bytes 393224 | tf_op jit(solution)/shard_map/ppermute | solution.py:217
  27.9 1.1 %collective-permute-start.6 = (f32[4,16,512]{2,1,0:T(8,128)S(1)}, f32[4,16,512]{2,1,0:T(8,128)S(1)}, u32[]{:S(2)}, u32[]{:S(2)}) collective-permute-start(f32[4,16,512]{2,1,0:T(8,128)S(1)} %get-tuple-element.23), channel_id=1, source_target_pairs={{0,2},{1,3},{2,0},{3,1},{4,6},{5,7},{6,4},{7,5},{8,10},{9,11},{10,... | collective-permute-start | bytes 393224 | tf_op jit(solution)/shard_map/ppermute | solution.py:217
  29.0 1.4 %collective-permute-start.7 = (f32[4,16,512]{2,1,0:T(8,128)S(1)}, f32[4,16,512]{2,1,0:T(8,128)S(1)}, u32[]{:S(2)}, u32[]{:S(2)}) collective-permute-start(f32[4,16,512]{2,1,0:T(8,128)S(1)} %get-tuple-element.24), channel_id=1, source_target_pairs={{0,3},{1,0},{2,1},{3,2},{4,7},{5,4},{6,5},{7,6},{8,11},{9,8},{10,9... | collective-permute-start | bytes 393224 | tf_op jit(solution)/shard_map/ppermute | solution.py:217
  30.3 1.6 %collective-permute-done.5.refs_1_ = f32[4,16,512]{2,1,0:T(8,128)S(1)} collective-permute-done((f32[4,16,512]{2,1,0:T(8,128)S(1)}, f32[4,16,512]{2,1,0:T(8,128)S(1)}, u32[]{:S(2)}, u32[]{:S(2)}) %collective-permute-start.5) | collective-permute-done | bytes 131104 | tf_op jit(solution)/shard_map/ppermute | solution.py:217
  31.9 7.5 %collective-permute-done.6.refs_2_ = f32[4,16,512]{2,1,0:T(8,128)S(1)} collective-permute-done((f32[4,16,512]{2,1,0:T(8,128)S(1)}, f32[4,16,512]{2,1,0:T(8,128)S(1)}, u32[]{:S(2)}, u32[]{:S(2)}) %collective-permute-start.6) | collective-permute-done | bytes 131104 | tf_op jit(solution)/shard_map/ppermute | solution.py:217
  39.5 1.9 %collective-permute-done.7.refs_3_ = f32[4,16,512]{2,1,0:T(8,128)S(1)} collective-permute-done((f32[4,16,512]{2,1,0:T(8,128)S(1)}, f32[4,16,512]{2,1,0:T(8,128)S(1)}, u32[]{:S(2)}, u32[]{:S(2)}) %collective-permute-start.7) | collective-permute-done | bytes 131104 | tf_op jit(solution)/shard_map/ppermute | solution.py:217
  41.3 0.0 copy-done.9
  41.3 1.3 %combine.1 = f32[4,16,512]{2,1,0:T(8,128)} custom-call(s32[1]{0:T(128)} %bitcast.mine_ref, s32[4]{0:T(128)S(1)} %copy-done.9, f32[4,16,512]{2,1,0:T(8,128)S(1)} %get-tuple-element.21.refs_0_, f32[4,16,512]{2,1,0:T(8,128)S(1)} %collective-permute-done.5.refs_1_, f32[4,16,512]{2,1,0:T(8,128)S(1)} %collective-permute-done.6.refs_2_, ...), custom_call_target="tpu_custom_call" | custom-call | tf_op jit(solution)/shard_map/combine/pallas_call | solution.py:219
  (13 shorter events, 0.1 us)
Async XLA Ops:
  0.0 1.2 %copy-start = (f32[16,8,2048]{2,1,0:T(8,128)S(1)}, f32[16,8,2048]{2,1,0:T(8,128)}, u32[]{:S(2)}) copy-start(f32[16,8,2048]{2,1,0:T(8,128)} %density_ref.3) | copy-start | bytes 3145732
  1.2 1.2 %copy-start.2 = (s32[16,8,2048]{2,1,0:T(8,128)S(1)}, s32[16,8,2048]{2,1,0:T(8,128)}, u32[]{:S(2)}) copy-start(s32[16,8,2048]{2,1,0:T(8,128)} %bin_ref.3) | copy-start | bytes 3145732
  2.5 0.7 %copy-start.7 = (f32[4,128]{1,0:T(4,128)S(1)}, f32[4,128]{1,0:T(4,128)}, u32[]{:S(2)}) copy-start(f32[4,128]{1,0:T(4,128)} %table_ref.3) | copy-start | bytes 6148
  3.1 12.3 %copy-start.1 = (f32[16,8,2048]{2,1,0:T(8,128)S(1)}, f32[16,8,2048]{2,1,0:T(8,128)}, u32[]{:S(2)}) copy-start(f32[16,8,2048]{2,1,0:T(8,128)} %density_ref.3) | copy-start | bytes 3145732
  3.1 12.3 %copy-start.3 = (s32[16,8,2048]{2,1,0:T(8,128)S(1)}, s32[16,8,2048]{2,1,0:T(8,128)}, u32[]{:S(2)}) copy-start(s32[16,8,2048]{2,1,0:T(8,128)} %bin_ref.3) | copy-start | bytes 3145732
  3.9 1.0 %copy-start.5 = (f32[16,8,2048]{2,1,0:T(8,128)}, f32[16,8,2048]{2,1,0:T(8,128)S(1)}, u32[]{:S(2)}) copy-start(f32[16,8,2048]{2,1,0:T(8,128)S(1)} %get-tuple-element.17.before_ref) | copy-start | bytes 3145732
  4.9 1.6 %collective-permute-start = (f32[8,2048]{1,0:T(8,128)S(1)}, f32[8,2048]{1,0:T(8,128)S(1)}, u32[]{:S(2)}, u32[]{:S(2)}) collective-permute-start(f32[8,2048]{1,0:T(8,128)S(1)} %get-tuple-element.15), channel_id=1, source_target_pairs={{0,4},{4,0},{8,12},{12,8},{16,20},{20,16},{24,28},{28,24},{1,5},{5... | collective-permute-start | bytes 196616 | tf_op jit(solution)/shard_map/ppermute | solution.py:183
  6.5 7.5 %collective-permute-start.1 = (f32[8,2048]{1,0:T(8,128)S(1)}, f32[8,2048]{1,0:T(8,128)S(1)}, u32[]{:S(2)}, u32[]{:S(2)}) collective-permute-start(f32[8,2048]{1,0:T(8,128)S(1)} %add.12), channel_id=1, source_target_pairs={{0,8},{4,12},{8,0},{12,4},{16,24},{20,28},{24,16},{28,20},{1,9},{5... | collective-permute-start | bytes 196616 | tf_op jit(solution)/shard_map/ppermute | solution.py:183
  8.4 7.0 %collective-permute-start.4 = (f32[8,2048]{1,0:T(8,128)}, f32[8,2048]{1,0:T(8,128)S(1)}, u32[]{:S(2)}, u32[]{:S(2)}) collective-permute-start(f32[8,2048]{1,0:T(8,128)} %get-tuple-element.25), channel_id=1, source_target_pairs={{4,0},{8,4},{12,8},{16,12},{20,16},{24,20},{28,24},{5,1},{9,5},{13... | collective-permute-start | bytes 196616 | tf_op jit(solution)/shard_map/ppermute | solution.py:168
  11.0 4.5 %collective-permute-start.3 = (f32[8,2048]{1,0:T(8,128)S(1)}, f32[8,2048]{1,0:T(8,128)S(1)}, u32[]{:S(2)}, u32[]{:S(2)}) collective-permute-start(f32[8,2048]{1,0:T(8,128)S(1)} %get-tuple-element.26), channel_id=1, source_target_pairs={{0,4},{4,8},{8,12},{12,16},{16,20},{20,24},{24,28},{1,5},{5,9},{9,... | collective-permute-start | bytes 196616 | tf_op jit(solution)/shard_map/ppermute | solution.py:167
  14.0 10.1 %collective-permute-start.2 = (f32[8,2048]{1,0:T(8,128)S(1)}, f32[8,2048]{1,0:T(8,128)S(1)}, u32[]{:S(2)}, u32[]{:S(2)}) collective-permute-start(f32[8,2048]{1,0:T(8,128)S(1)} %add.14), channel_id=1, source_target_pairs={{0,16},{4,20},{8,24},{12,28},{16,0},{20,4},{24,8},{28,12},{1,17},{... | collective-permute-start | bytes 196616 | tf_op jit(solution)/shard_map/ppermute | solution.py:183
  15.4 1.2 %copy-start.6 = (f32[16,8,2048]{2,1,0:T(8,128)S(1)}, f32[16,8,2048]{2,1,0:T(8,128)}, u32[]{:S(2)}) copy-start(f32[16,8,2048]{2,1,0:T(8,128)} %copy-done.5) | copy-start | bytes 3145732
  16.7 0.7 %copy-start.8 = (f32[4,128]{1,0:T(4,128)S(1)}, f32[4,128]{1,0:T(4,128)}, u32[]{:S(2)}) copy-start(f32[4,128]{1,0:T(4,128)} %table_ref.3) | copy-start | bytes 6148
  17.3 24.0 %copy-start.9 = (s32[4]{0:T(128)S(1)}, s32[4]{0:T(128)}, u32[]{:S(2)}) copy-start(s32[4]{0:T(128)} %order_ref.1) | copy-start | bytes 52
  24.1 1.9 %copy-start.4 = (f32[3,8,16,2048]{3,2,1,0:T(8,128)S(1)}, f32[3,8,16,2048]{3,2,1,0:T(8,128)}, u32[]{:S(2)}) copy-start(f32[3,8,16,2048]{3,2,1,0:T(8,128)} %get-tuple-element.18.lit_ref) | copy-start | bytes 9437188
  26.5 5.4 %collective-permute-start.5 = (f32[4,16,512]{2,1,0:T(8,128)S(1)}, f32[4,16,512]{2,1,0:T(8,128)S(1)}, u32[]{:S(2)}, u32[]{:S(2)}) collective-permute-start(f32[4,16,512]{2,1,0:T(8,128)S(1)} %get-tuple-element.22), channel_id=1, source_target_pairs={{0,1},{1,2},{2,3},{3,0},{4,5},{5,6},{6,7},{7,4},{8,9},{9,10},{10,1... | collective-permute-start | bytes 393224 | tf_op jit(solution)/shard_map/ppermute | solution.py:217
  27.9 11.6 %collective-permute-start.6 = (f32[4,16,512]{2,1,0:T(8,128)S(1)}, f32[4,16,512]{2,1,0:T(8,128)S(1)}, u32[]{:S(2)}, u32[]{:S(2)}) collective-permute-start(f32[4,16,512]{2,1,0:T(8,128)S(1)} %get-tuple-element.23), channel_id=1, source_target_pairs={{0,2},{1,3},{2,0},{3,1},{4,6},{5,7},{6,4},{7,5},{8,10},{9,11},{10,... | collective-permute-start | bytes 393224 | tf_op jit(solution)/shard_map/ppermute | solution.py:217
  29.0 12.4 %collective-permute-start.7 = (f32[4,16,512]{2,1,0:T(8,128)S(1)}, f32[4,16,512]{2,1,0:T(8,128)S(1)}, u32[]{:S(2)}, u32[]{:S(2)}) collective-permute-start(f32[4,16,512]{2,1,0:T(8,128)S(1)} %get-tuple-element.24), channel_id=1, source_target_pairs={{0,3},{1,0},{2,1},{3,2},{4,7},{5,4},{6,5},{7,6},{8,11},{9,8},{10,9... | collective-permute-start | bytes 393224 | tf_op jit(solution)/shard_map/ppermute | solution.py:217

commit v2 on v0

v2 whole, which is shorter than its diff:
```python
import functools

import jax
import jax.numpy as jnp
from jax import lax
from jax.experimental import pallas as pl
from jax.experimental.pallas import tpu as pltpu
from jax.sharding import PartitionSpec as P

AMBIENT = 0.25
LANES = 128
LOG2E = 1.4426950408889634
F32 = jnp.float32


def table_rows(table_ref, channel):
    entries = table_ref.shape[1]
    return [
        jnp.broadcast_to(table_ref[channel : channel + 1, first : first + LANES], (8, LANES))
        for first in range(0, entries, LANES)
    ]


def look_up(rows, index):
    low = index if len(rows) == 1 else index & (LANES - 1)
    value = jnp.take_along_axis(rows[0], low, axis=1)
    for part in range(1, len(rows)):
        value = jnp.where(index >= part * LANES, jnp.take_along_axis(rows[part], low, axis=1), value)
    return value


def lanes(tile):
    return slice(tile * LANES, (tile + 1) * LANES)


def eight(i):
    return pl.ds(pl.multiple_of(i * 8, 8), 8)


def extinction_kernel(
    tiles_along, density_hbm, bin_hbm, table_hbm, order_hbm,
    density_ref, table_ref, entry_ref, ext_ref, send_ref, edge_ref, front_ref,
    bin_ref, order_ref, density_sem, bin_sem, table_sem, order_sem,
):
    light_cells, _, columns = density_hbm.shape
    tiles = columns // LANES
    table_copy = pltpu.make_async_copy(table_hbm, table_ref, table_sem)
    table_copy.start()
    order_copy = pltpu.make_async_copy(order_hbm, order_ref, order_sem)
    order_copy.start()
    parts = 2
    size = light_cells // parts
    copies = []
    for part in range(parts):
        at = slice(part * size, (part + 1) * size)
        first = pltpu.make_async_copy(bin_hbm.at[at], bin_ref.at[at], bin_sem.at[part])
        second = pltpu.make_async_copy(density_hbm.at[at], density_ref.at[at], density_sem.at[part])
        first.start()
        second.start()
        copies.append((first, second))
    order_copy.wait()
    mine = lax.axis_index("tile")
    rank = [order_ref[lax.rem(mine - step + tiles_along, tiles_along)] for step in range(tiles_along)]
    for step in range(tiles_along):
        for other in range(tiles_along):
            front = jnp.where(rank[other] < rank[step], 1.0, 0.0)
            front_ref[step * tiles_along + other] = jnp.full((8, LANES), front, F32)
    table_copy.wait()
    rows = table_rows(table_ref, 3)
    running = tuple(jnp.zeros((8, LANES), F32) for _ in range(tiles))

    def layer(i, running):
        sums = []
        for tile in range(tiles):
            entry = bin_ref[i, :, lanes(tile)]
            ext = look_up(rows, entry) * density_ref[i, :, lanes(tile)]
            entry_ref[tile, eight(i)] = entry
            ext_ref[tile, eight(i)] = ext
            sums.append(running[tile] + ext)
        return tuple(sums)

    for part, (first, second) in enumerate(copies):
        first.wait()
        second.wait()
        running = lax.fori_loop(part * size, (part + 1) * size, layer, running, unroll=min(4, size))
    for tile in range(tiles):
        send_ref[0, :, lanes(tile)] = running[tile]
    odd = lax.rem(lax.axis_index("light"), 2)
    send_ref[1] = density_ref[(1 - odd) * (light_cells - 1)]
    edge_ref[...] = density_ref[odd * (light_cells - 1)]


def terms_kernel(view_step, table_ref, entry_ref, ext_ref, term_ref, clear_ref):
    _, depth_cells, light_cells, columns = term_ref.shape
    tables = [table_rows(table_ref, c) for c in range(3)]

    @pl.loop(0, columns // LANES, unroll=2)
    def _(tile):
        at = pl.ds(pl.multiple_of(tile * LANES, LANES), LANES)
        for half in range(0, light_cells, 8):
            clear = jnp.ones((8, LANES), F32)
            for j in range(depth_cells):
                cells = pl.ds(half * depth_cells + j, 8, stride=depth_cells)
                further = clear * jnp.exp2(ext_ref[tile, cells] * (-view_step * LOG2E))
                weight = clear - further
                clear = further
                entry = entry_ref[tile, cells]
                for c in range(3):
                    term_ref[c, j, half : half + 8, at] = weight * look_up(tables[c], entry)
            clear_ref[half : half + 8, at] = clear


def shade_kernel(light_step, density_ref, ext_ref, pair_ref, edge_ref, shade_ref):
    light_cells, _, columns = density_ref.shape
    odd = lax.rem(lax.axis_index("light"), 2) == 1
    lane = lax.broadcasted_iota(jnp.int32, (8, LANES), 1)
    zero = jnp.zeros((8, LANES), F32)
    count = columns // LANES

    def layer(i, before, above, below):
        after = []
        cells = [density_ref[i, :, lanes(tile)] for tile in range(count)]
        up = [pltpu.roll(value, 1, 1) for value in cells]
        down = [pltpu.roll(value, LANES - 1, 1) for value in cells]
        for tile in range(count):
            left = jnp.where(lane == 0, up[tile - 1] if tile else zero, up[tile])
            right = jnp.where(lane == LANES - 1, down[tile + 1] if tile < count - 1 else zero, down[tile])
            slope = 0.5 * ((below(tile) - above(tile)) + (right - left))
            fade = jnp.exp2(before[tile] * (-light_step * LOG2E))
            after.append(before[tile] + ext_ref[tile, eight(i)])
            shade_ref[tile, eight(i)] = fade * (1.0 + 0.5 * jnp.tanh(slope))
        return tuple(after)

    def inside(i):
        return lambda tile: density_ref[i, :, lanes(tile)]

    def outside(when_odd, when_even):
        return lambda tile: jnp.where(odd, when_odd(lanes(tile)), when_even(lanes(tile)))

    from_pair = lambda at: pair_ref[1, :, at]
    from_edge = lambda at: edge_ref[:, at]
    last = light_cells - 1
    before = layer(0, (zero,) * count, outside(from_pair, from_edge), inside(1))
    before = lax.fori_loop(1, last, lambda i, b: layer(i, b, inside(i - 1), inside(i + 1)), before, unroll=2)
    layer(last, before, inside(last - 1), outside(from_edge, from_pair))


def picture_kernel(light_step, tiles, shade_ref, term_ref, clear_ref, pair_ref, *refs):
    group_refs, out_refs, fade_ref = refs[: -tiles - 1], refs[-tiles - 1 : -1], refs[-1]
    _, depth_cells, light_cells, columns = term_ref.shape
    share = columns // tiles
    mine = lax.axis_index("tile")
    place = lax.axis_index("light")
    upstream = jnp.where((place & 1) > 0, pair_ref[0], 0.0)
    for level, group_ref in enumerate(group_refs):
        upstream = upstream + jnp.where((place & (2 << level)) > 0, group_ref[...], 0.0)
    fade_ref[...] = jnp.exp2(upstream * (-light_step * LOG2E))
    for step, out_ref in enumerate(out_refs):
        owner = lax.rem(mine + step, tiles)
        for tile in range(share // LANES):
            at = pl.ds(pl.multiple_of(owner * share + tile * LANES, LANES), LANES)
            for half in range(0, light_cells, 8):
                rows = slice(half, half + 8)
                sums = [jnp.zeros((8, LANES), F32) for _ in range(3)]
                for j in range(depth_cells):
                    fade = jnp.broadcast_to(fade_ref[j : j + 1, at], (8, LANES))
                    cells = pl.ds(half * depth_cells + j, 8, stride=depth_cells)
                    light = AMBIENT + fade * shade_ref[owner * (share // LANES) + tile, cells]
                    for c in range(3):
                        sums[c] = sums[c] + light * term_ref[c, j, rows, at]
                for c in range(3):
                    out_ref[c, rows, lanes(tile)] = sums[c]
                out_ref[3, rows, lanes(tile)] = clear_ref[rows, at]


def combine_kernel(front_ref, *refs):
    *in_refs, out_ref = refs
    steps = range(len(in_refs))
    _, light_cells, share = out_ref.shape
    for half in range(0, light_cells, 8):
        for tile in range(share // LANES):
            at = (slice(half, half + 8), lanes(tile))
            clear = [ref[3, *at] for ref in in_refs]
            sums = [jnp.zeros((8, LANES), F32) for _ in range(3)]
            through = clear[0]
            for step in steps[1:]:
                through = through * clear[step]
            for step in steps:
                ahead = jnp.ones((8, LANES), F32)
                for other in steps:
                    if other != step:
                        ahead = ahead * jnp.where(front_ref[step * len(steps) + other] > 0.5, clear[other], 1.0)
                for c in range(3):
                    sums[c] = sums[c] + ahead * in_refs[step][c, *at]
            for c in range(3):
                out_ref[c, *at] = sums[c]
            out_ref[3, *at] = 1.0 - through


def call(kernel, outs, ins, name, scratch=(), cost=1.0):
    cycles = int(cost * 1000)
    return pl.pallas_call(
        kernel,
        out_shape=outs,
        in_specs=[pl.BlockSpec(memory_space=pltpu.VMEM)] * len(ins),
        out_specs=jax.tree.map(lambda _: pl.BlockSpec(memory_space=pltpu.VMEM), outs),
        scratch_shapes=list(scratch),
        compiler_params=pltpu.CompilerParams(vmem_limit_bytes=8 * 2**20),
        cost_estimate=pl.CostEstimate(flops=cycles * 1000, bytes_accessed=cycles * 3000, transcendentals=0),
        name=name,
    )(*ins)


def per_device(density, bin_index, transfer, depth_order):
    light_cells, depth_cells, columns = density.shape
    light_count = lax.axis_size("light")
    tile_count = lax.axis_size("tile")
    light_step = 3.0 / (light_cells * light_count)
    view_step = 3.0 / (depth_cells * tile_count)
    share = columns // tile_count

    def shape(*dims, dtype=F32):
        return jax.ShapeDtypeStruct(dims, dtype)

    plane = shape(depth_cells, columns)
    tiled = (columns // LANES, light_cells * depth_cells, LANES)
    hbm = pl.BlockSpec(memory_space=pltpu.HBM)
    vmem = pl.BlockSpec(memory_space=pltpu.VMEM)
    outs = [
        shape(*density.shape), shape(*transfer.shape), shape(*tiled, dtype=jnp.int32), shape(*tiled),
        shape(2, *plane.shape), plane, shape(tile_count * tile_count, 8, LANES),
    ]
    dense, table, entry, ext, send, edge, front = pl.pallas_call(
        functools.partial(extinction_kernel, tile_count),
        out_shape=outs,
        in_specs=[hbm] * 4,
        out_specs=[vmem] * len(outs),
        scratch_shapes=[
            pltpu.VMEM(bin_index.shape, jnp.int32),
            pltpu.SMEM(depth_order.shape, jnp.int32),
            pltpu.SemaphoreType.DMA((2,)),
            pltpu.SemaphoreType.DMA((2,)),
            pltpu.SemaphoreType.DMA,
            pltpu.SemaphoreType.DMA,
        ],
        compiler_params=pltpu.CompilerParams(vmem_limit_bytes=8 * 2**20),
        name="extinction",
    )(*[pltpu.with_memory_space_constraint(a, pltpu.HBM) for a in (density, bin_index, transfer, depth_order)])

    pair = lax.ppermute(send, "light", [(i, i ^ 1) for i in range(light_count)])
    beside = [(i, i + 1) for i in range(1, light_count - 1, 2)]
    edge = lax.ppermute(edge, "light", beside + [(b, a) for a, b in beside])
    term, clear = call(
        functools.partial(terms_kernel, view_step),
        [shape(3, depth_cells, light_cells, columns), shape(light_cells, columns)],
        (table, entry, ext), "terms", cost=2.5,
    )
    shade = call(
        functools.partial(shade_kernel, light_step), shape(*tiled), (dense, ext, pair, edge), "shade", cost=1.2
    )
    group = send[0] + pair[0]
    groups = []
    step = 2
    while step < light_count:
        if step == light_count // 2:
            group, shade = lax.optimization_barrier((group, shade))
        got = lax.ppermute(group, "light", [(i, i ^ step) for i in range(light_count)])
        groups.append(got)
        group = group + got
        step *= 2
    pieces = call(
        functools.partial(picture_kernel, light_step, tile_count),
        [shape(4, light_cells, share)] * tile_count,
        (shade, term, clear, pair, *groups), "picture",
        scratch=[pltpu.VMEM(plane.shape, F32)], cost=0.6,
    )
    held = [pieces[0]]
    for step in range(1, tile_count):
        held.append(
            lax.ppermute(pieces[step], "tile", [(i, (i + step) % tile_count) for i in range(tile_count)])
        )
    return call(combine_kernel, shape(4, light_cells, share), (front, *held), "combine")


def solution(mesh):
    in_specs = (P("light", "tile", None), P("light", "tile", None), P(), P())
    out_specs = P(None, "light", "tile")
    return jax.shard_map(
        per_device, mesh=mesh, in_specs=in_specs, out_specs=out_specs, check_vma=False
    )
```

time: 1030 us -> 31.2 us (0.03)
  the two profiles are of different devices: /device:TPU:0 before, /device:TPU:11 now
where the time goes in v2:
time: 31.2 us; the launch traced here: 31.1 us
  waiting for transfers between devices  16 us (51%)
  starting transfers between devices  7.98 us (26%)
  Pallas kernels  7.04 us (23%)
    ppermute x3, waiting for transfers between devices, per_device(): lax.ppermute(pieces[step], 'tile', [(i, (i + step) % tile_count) for i in...  10.9 us
    pallas_call x4, Pallas kernels, call(): pl.pallas_call(kernel, out_shape=outs, in_specs=[pl.BlockSpec(memory_spac...  4.76 us
    ppermute x3, starting transfers between devices, per_device(): lax.ppermute(pieces[step], 'tile', [(i, (i + step) % tile_count) for i in...  3.83 us
    ppermute x1, waiting for transfers between devices, per_device(): edge = lax.ppermute(edge, 'light', beside + [(b, a) for a, b in beside])  3.74 us
    ppermute x1, starting transfers between devices, per_device(): edge = lax.ppermute(edge, 'light', beside + [(b, a) for a, b in beside])  3.02 us
    pallas_call x1, Pallas kernels, per_device(): pl.pallas_call(functools.partial(extinction_kernel, tile_count), out_shap...  2.27 us
    ppermute x2, waiting for transfers between devices, per_device(): lax.ppermute(group, 'light', [(i, i ^ step) for i in range(light_count)])  1.31 us
    ppermute x1, starting transfers between devices, per_device(): pair = lax.ppermute(send, 'light', [(i, i ^ 1) for i in range(light_count)])  0.74 us
  transfers between devices with their start and end apart: 7, of which 5 were waited for; matrix products, arithmetic and copies ran while one was open for 0% of the time, Pallas kernels for 11%

profile of v2, /device:TPU:11, one launch (start us, length us, event | category | flops | bytes accessed | tf_op | source)
XLA Modules:
  0.0 31.1 jit_solution(1779577161040583579)
XLA Ops:
  0.0 2.3 %extinction.1 = (f32[16,8,2048]{2,1,0:T(8,128)S(1)}, f32[4,128]{1,0:T(4,128)S(1)}, s32[16,128,128]{2,1,0:T(8,128)S(1)}, f32[16,128,128]{2,1,0:T(8,128)S(1)}, f32...) custom-call(f32[16,8,2048]{2,1,0:T(8,128)} %density_hbm.1, s32[16,8,2048]{2,1,0:T(8,128)} %bin_hbm.1, ...), custom_call_target="tpu_custom_call" | custom-call | tf_op jit(solution)/shard_map/extinction/pallas_call | solution.py:233
  2.3 0.7 %collective-permute-start = (f32[2,8,2048]{2,1,0:T(8,128)S(1)}, f32[2,8,2048]{2,1,0:T(8,128)S(1)}, u32[]{:S(2)}, u32[]{:S(2)}) collective-permute-start(f32[2,8,2048]{2,1,0:T(8,128)S(1)} %get-tuple-element.21), channel_id=1, source_target_pairs={{0,4},{4,0},{8,12},{12,8},{16,20},{20,16},{24,28},{28,24},{1,5},{5... | collective-permute-start | bytes 393224 | tf_op jit(solution)/shard_map/ppermute | solution.py:250
  3.0 3.0 %collective-permute-start.2 = (f32[8,2048]{1,0:T(8,128)S(1)}, f32[8,2048]{1,0:T(8,128)S(1)}, u32[]{:S(2)}, u32[]{:S(2)}) collective-permute-start(f32[8,2048]{1,0:T(8,128)S(1)} %get-tuple-element.24), channel_id=1, source_target_pairs={{4,8},{12,16},{20,24},{8,4},{16,12},{24,20},{5,9},{13,17},{21,25},... | collective-permute-start | bytes 196616 | tf_op jit(solution)/shard_map/ppermute | solution.py:252
  6.0 0.0 collective-permute-done.pair_ref
  6.1 0.3 %collective-permute-start.1 = (f32[8,2048]{1,0:T(8,128)S(1)}, f32[8,2048]{1,0:T(8,128)S(1)}, u32[]{:S(2)}, u32[]{:S(2)}) collective-permute-start(f32[8,2048]{1,0:T(8,128)S(1)} %fusion), channel_id=1, source_target_pairs={{0,8},{4,12},{8,0},{12,4},{16,24},{20,28},{24,16},{28,20},{1,9},{5... | collective-permute-start | bytes 196616 | tf_op jit(solution)/shard_map/ppermute | solution.py:267
  6.4 3.7 %collective-permute-done.2.edge_ref = f32[8,2048]{1,0:T(8,128)S(1)} collective-permute-done((f32[8,2048]{1,0:T(8,128)S(1)}, f32[8,2048]{1,0:T(8,128)S(1)}, u32[]{:S(2)}, u32[]{:S(2)}) %collective-permute-start.2) | collective-permute-done | bytes 65568 | tf_op jit(solution)/shard_map/ppermute | solution.py:252
  10.1 1.3 %shade.1.shade_ref = f32[16,128,128]{2,1,0:T(8,128)S(1)} custom-call(f32[16,8,2048]{2,1,0:T(8,128)S(1)} %get-tuple-element.22.density_ref, f32[16,128,128]{2,1,0:T(8,128)S(1)} %get-tuple-element.23.ext_ref, f32[2,8,2048]{2,1,0:T(8,128)S(1)} %collective-permute-done.pair_ref, f32[8,2048]{1,0:T(8,128)S(1)} %collective-permute-done.2.edge_ref), custom_call_target="tpu_custom_call" | custom-call | flops 1200000 | bytes 3600000 | tf_op jit(solution)/shard_map/shade/pallas_call | solution.py:202
  11.4 0.0 collective-permute-done.1.refs_0_
  11.5 0.1 collective-permute-start.3
  11.5 2.2 %terms.1 = (f32[3,8,16,2048]{3,2,1,0:T(8,128)S(1)}, f32[16,2048]{1,0:T(8,128)S(1)}) custom-call(f32[4,128]{1,0:T(4,128)S(1)} %get-tuple-element.26.table_ref, s32[16,128,128]{2,1,0:T(8,128)S(1)} %get-tuple-element.27.entry_ref, f32[16,128,128]{2,1,0:T(8,128)S(1)} %get-tuple-element.23.ext_ref), custom_call_target="tpu_custom_call" | custom-call | flops 2500000 | bytes 7500000 | tf_op jit(solution)/shard_map/terms/pallas_call | solution.py:202
  13.7 1.3 %collective-permute-done.3.refs_1_ = f32[8,2048]{1,0:T(8,128)S(1)} collective-permute-done((f32[8,2048]{1,0:T(8,128)S(1)}, f32[8,2048]{1,0:T(8,128)S(1)}, u32[]{:S(2)}, u32[]{:S(2)}) %collective-permute-start.3) | collective-permute-done | bytes 65568 | tf_op jit(solution)/shard_map/ppermute | solution.py:267
  15.0 0.6 %picture.1 = (f32[4,16,512]{2,1,0:T(8,128)S(1)}, f32[4,16,512]{2,1,0:T(8,128)S(1)}, f32[4,16,512]{2,1,0:T(8,128)S(1)}, f32[4,16,512]{2,1,0:T(8,128)S(1)}) custom-call(f32[16,128,128]{2,1,0:T(8,128)S(1)} %shade.1.shade_ref, f32[3,8,16,2048]{3,2,1,0:T(8,128)S(1)} %get-tuple-element.28.term_ref, f32[16,2048]{1,0:T(8,128)S(1)} %get-tuple-element.29.clear_ref, ...), custom_call_target="tpu_custom_call" | custom-call | flops 600000 | bytes 1800000 | tf_op jit(solution)/shard_map/picture/pallas_call | solution.py:202
  15.6 1.3 %collective-permute-start.4 = (f32[4,16,512]{2,1,0:T(8,128)S(1)}, f32[4,16,512]{2,1,0:T(8,128)S(1)}, u32[]{:S(2)}, u32[]{:S(2)}) collective-permute-start(f32[4,16,512]{2,1,0:T(8,128)S(1)} %get-tuple-element.32), channel_id=1, source_target_pairs={{0,1},{1,2},{2,3},{3,0},{4,5},{5,6},{6,7},{7,4},{8,9},{9,10},{10,1... | collective-permute-start | bytes 393224 | tf_op jit(solution)/shard_map/ppermute | solution.py:280
  17.0 1.1 %collective-permute-start.5 = (f32[4,16,512]{2,1,0:T(8,128)S(1)}, f32[4,16,512]{2,1,0:T(8,128)S(1)}, u32[]{:S(2)}, u32[]{:S(2)}) collective-permute-start(f32[4,16,512]{2,1,0:T(8,128)S(1)} %get-tuple-element.33), channel_id=1, source_target_pairs={{0,2},{1,3},{2,0},{3,1},{4,6},{5,7},{6,4},{7,5},{8,10},{9,11},{10,... | collective-permute-start | bytes 393224 | tf_op jit(solution)/shard_map/ppermute | solution.py:280
  18.1 1.4 %collective-permute-start.6 = (f32[4,16,512]{2,1,0:T(8,128)S(1)}, f32[4,16,512]{2,1,0:T(8,128)S(1)}, u32[]{:S(2)}, u32[]{:S(2)}) collective-permute-start(f32[4,16,512]{2,1,0:T(8,128)S(1)} %get-tuple-element.34), channel_id=1, source_target_pairs={{0,3},{1,0},{2,1},{3,2},{4,7},{5,4},{6,5},{7,6},{8,11},{9,8},{10,9... | collective-permute-start | bytes 393224 | tf_op jit(solution)/shard_map/ppermute | solution.py:280
  19.4 0.9 %collective-permute-done.4.refs_1_ = f32[4,16,512]{2,1,0:T(8,128)S(1)} collective-permute-done((f32[4,16,512]{2,1,0:T(8,128)S(1)}, f32[4,16,512]{2,1,0:T(8,128)S(1)}, u32[]{:S(2)}, u32[]{:S(2)}) %collective-permute-start.4) | collective-permute-done | bytes 131104 | tf_op jit(solution)/shard_map/ppermute | solution.py:280
  20.4 7.5 %collective-permute-done.5.refs_2_ = f32[4,16,512]{2,1,0:T(8,128)S(1)} collective-permute-done((f32[4,16,512]{2,1,0:T(8,128)S(1)}, f32[4,16,512]{2,1,0:T(8,128)S(1)}, u32[]{:S(2)}, u32[]{:S(2)}) %collective-permute-start.5) | collective-permute-done | bytes 131104 | tf_op jit(solution)/shard_map/ppermute | solution.py:280
  27.9 2.5 %collective-permute-done.6.refs_3_ = f32[4,16,512]{2,1,0:T(8,128)S(1)} collective-permute-done((f32[4,16,512]{2,1,0:T(8,128)S(1)}, f32[4,16,512]{2,1,0:T(8,128)S(1)}, u32[]{:S(2)}, u32[]{:S(2)}) %collective-permute-start.6) | collective-permute-done | bytes 131104 | tf_op jit(solution)/shard_map/ppermute | solution.py:280
  30.4 0.7 %combine.1 = f32[4,16,512]{2,1,0:T(8,128)} custom-call(f32[16,8,128]{2,1,0:T(8,128)S(1)} %get-tuple-element.20.front_ref, f32[4,16,512]{2,1,0:T(8,128)S(1)} %get-tuple-element.31.refs_0_, f32[4,16,512]{2,1,0:T(8,128)S(1)} %collective-permute-done.4.refs_1_, f32[4,16,512]{2,1,0:T(8,128)S(1)} %collective-permute-done.5.refs_2_, ...), custom_call_target="tpu_custom_call" | custom-call | flops 1000000 | bytes 3000000 | tf_op jit(solution)/shard_map/combine/pallas_call | solution.py:202
  (2 shorter events, 0.0 us)
Async XLA Ops:
  2.3 3.8 %collective-permute-start = (f32[2,8,2048]{2,1,0:T(8,128)S(1)}, f32[2,8,2048]{2,1,0:T(8,128)S(1)}, u32[]{:S(2)}, u32[]{:S(2)}) collective-permute-start(f32[2,8,2048]{2,1,0:T(8,128)S(1)} %get-tuple-element.21), channel_id=1, source_target_pairs={{0,4},{4,0},{8,12},{12,8},{16,20},{20,16},{24,28},{28,24},{1,5},{5... | collective-permute-start | bytes 393224 | tf_op jit(solution)/shard_map/ppermute | solution.py:250
  3.0 7.1 %collective-permute-start.2 = (f32[8,2048]{1,0:T(8,128)S(1)}, f32[8,2048]{1,0:T(8,128)S(1)}, u32[]{:S(2)}, u32[]{:S(2)}) collective-permute-start(f32[8,2048]{1,0:T(8,128)S(1)} %get-tuple-element.24), channel_id=1, source_target_pairs={{4,8},{12,16},{20,24},{8,4},{16,12},{24,20},{5,9},{13,17},{21,25},... | collective-permute-start | bytes 196616 | tf_op jit(solution)/shard_map/ppermute | solution.py:252
  6.1 5.4 %collective-permute-start.1 = (f32[8,2048]{1,0:T(8,128)S(1)}, f32[8,2048]{1,0:T(8,128)S(1)}, u32[]{:S(2)}, u32[]{:S(2)}) collective-permute-start(f32[8,2048]{1,0:T(8,128)S(1)} %fusion), channel_id=1, source_target_pairs={{0,8},{4,12},{8,0},{12,4},{16,24},{20,28},{24,16},{28,20},{1,9},{5... | collective-permute-start | bytes 196616 | tf_op jit(solution)/shard_map/ppermute | solution.py:267
  11.5 3.5 %collective-permute-start.3 = (f32[8,2048]{1,0:T(8,128)S(1)}, f32[8,2048]{1,0:T(8,128)S(1)}, u32[]{:S(2)}, u32[]{:S(2)}) collective-permute-start(f32[8,2048]{1,0:T(8,128)S(1)} %add.11), channel_id=1, source_target_pairs={{0,16},{4,20},{8,24},{12,28},{16,0},{20,4},{24,8},{28,12},{1,17},{... | collective-permute-start | bytes 196616 | tf_op jit(solution)/shard_map/ppermute | solution.py:267
  15.6 4.7 %collective-permute-start.4 = (f32[4,16,512]{2,1,0:T(8,128)S(1)}, f32[4,16,512]{2,1,0:T(8,128)S(1)}, u32[]{:S(2)}, u32[]{:S(2)}) collective-permute-start(f32[4,16,512]{2,1,0:T(8,128)S(1)} %get-tuple-element.32), channel_id=1, source_target_pairs={{0,1},{1,2},{2,3},{3,0},{4,5},{5,6},{6,7},{7,4},{8,9},{9,10},{10,1... | collective-permute-start | bytes 393224 | tf_op jit(solution)/shard_map/ppermute | solution.py:280
  17.0 10.9 %collective-permute-start.5 = (f32[4,16,512]{2,1,0:T(8,128)S(1)}, f32[4,16,512]{2,1,0:T(8,128)S(1)}, u32[]{:S(2)}, u32[]{:S(2)}) collective-permute-start(f32[4,16,512]{2,1,0:T(8,128)S(1)} %get-tuple-element.33), channel_id=1, source_target_pairs={{0,2},{1,3},{2,0},{3,1},{4,6},{5,7},{6,4},{7,5},{8,10},{9,11},{10,... | collective-permute-start | bytes 393224 | tf_op jit(solution)/shard_map/ppermute | solution.py:280
  18.1 12.3 %collective-permute-start.6 = (f32[4,16,512]{2,1,0:T(8,128)S(1)}, f32[4,16,512]{2,1,0:T(8,128)S(1)}, u32[]{:S(2)}, u32[]{:S(2)}) collective-permute-start(f32[4,16,512]{2,1,0:T(8,128)S(1)} %get-tuple-element.34), channel_id=1, source_target_pairs={{0,3},{1,0},{2,1},{3,2},{4,7},{5,4},{6,5},{7,6},{8,11},{9,8},{10,9... | collective-permute-start | bytes 393224 | tf_op jit(solution)/shard_map/ppermute | solution.py:280

commit v3 on v2

--- a/solution.py
+++ b/solution.py
@@ -110,39 +110,72 @@
             clear_ref[half : half + 8, at] = clear
 
 
-def shade_kernel(light_step, density_ref, ext_ref, pair_ref, edge_ref, shade_ref):
-    light_cells, _, columns = density_ref.shape
-    odd = lax.rem(lax.axis_index("light"), 2) == 1
+def shaded(light_step, cells, before, above, below):
     lane = lax.broadcasted_iota(jnp.int32, (8, LANES), 1)
     zero = jnp.zeros((8, LANES), F32)
+    up = [pltpu.roll(value, 1, 1) for value in cells]
+    down = [pltpu.roll(value, LANES - 1, 1) for value in cells]
+    result = []
+    for tile in range(len(cells)):
+        left = jnp.where(lane == 0, up[tile - 1] if tile else zero, up[tile])
+        right = jnp.where(lane == LANES - 1, down[tile + 1] if tile < len(cells) - 1 else zero, down[tile])
+        slope = 0.5 * ((below(tile) - above(tile)) + (right - left))
+        fade = jnp.exp2(before[tile] * (-light_step * LOG2E))
+        result.append(fade * (1.0 + 0.5 * jnp.tanh(slope)))
+    return result
+
+
+def shade_kernel(light_step, density_ref, ext_ref, shade_ref):
+    light_cells, _, columns = density_ref.shape
     count = columns // LANES
 
-    def layer(i, before, above, below):
-        after = []
-        cells = [density_ref[i, :, lanes(tile)] for tile in range(count)]
-        up = [pltpu.roll(value, 1, 1) for value in cells]
-        down = [pltpu.roll(value, LANES - 1, 1) for value in cells]
+    def layer(i, before):
+        values = shaded(
+            light_step,
+            [density_ref[i, :, lanes(tile)] for tile in range(count)],
+            before,
+            lambda tile: density_ref[i - 1, :, lanes(tile)],
+            lambda tile: density_ref[i + 1, :, lanes(tile)],
+        )
         for tile in range(count):
-            left = jnp.where(lane == 0, up[tile - 1] if tile else zero, up[tile])
-            right = jnp.where(lane == LANES - 1, down[tile + 1] if tile < count - 1 else zero, down[tile])
-            slope = 0.5 * ((below(tile) - above(tile)) + (right - left))
-            fade = jnp.exp2(before[tile] * (-light_step * LOG2E))
-            after.append(before[tile] + ext_ref[tile, eight(i)])
-            shade_ref[tile, eight(i)] = fade * (1.0 + 0.5 * jnp.tanh(slope))
-        return tuple(after)
-
-    def inside(i):
-        return lambda tile: density_ref[i, :, lanes(tile)]
-
-    def outside(when_odd, when_even):
-        return lambda tile: jnp.where(odd, when_odd(lanes(tile)), when_even(lanes(tile)))
-
-    from_pair = lambda at: pair_ref[1, :, at]
-    from_edge = lambda at: edge_ref[:, at]
+            shade_ref[tile, eight(i)] = values[tile]
+        return tuple(before[tile] + ext_ref[tile, eight(i)] for tile in range(count))
+
+    for tile in range(count):
+        shade_ref[tile, eight(0)] = jnp.zeros((8, LANES), F32)
+        shade_ref[tile, eight(light_cells - 1)] = jnp.zeros((8, LANES), F32)
+    before = tuple(ext_ref[tile, eight(0)] for tile in range(count))
+    lax.fori_loop(1, light_cells - 1, layer, before, unroll=2)
+
+
+def outer_kernel(light_step, light_count, density_ref, ext_ref, send_ref, pair_ref, edge_ref, _, shade_ref):
+    light_cells, _, columns = density_ref.shape
+    count = columns // LANES
+    place = lax.axis_index("light")
+    odd = lax.rem(place, 2) == 1
+    inner = jnp.logical_and(place > 0, place < light_count - 1)
     last = light_cells - 1
-    before = layer(0, (zero,) * count, outside(from_pair, from_edge), inside(1))
-    before = lax.fori_loop(1, last, lambda i, b: layer(i, b, inside(i - 1), inside(i + 1)), before, unroll=2)
-    layer(last, before, inside(last - 1), outside(from_edge, from_pair))
+
+    def beside(tile, pair_here):
+        edge = jnp.where(inner, edge_ref[:, lanes(tile)], 0.0)
+        return jnp.where(pair_here, pair_ref[1, :, lanes(tile)], edge)
+
+    zero = jnp.zeros((8, LANES), F32)
+    first = shaded(
+        light_step, [density_ref[0, :, lanes(tile)] for tile in range(count)], [zero] * count,
+        lambda tile: beside(tile, odd),
+        lambda tile: density_ref[1, :, lanes(tile)],
+    )
+    for tile in range(count):
+        shade_ref[tile, 0:8] = first[tile]
+    final = shaded(
+        light_step, [density_ref[last, :, lanes(tile)] for tile in range(count)],
+        [send_ref[0, :, lanes(tile)] - ext_ref[tile, last * 8 : last * 8 + 8] for tile in range(count)],
+        lambda tile: density_ref[last - 1, :, lanes(tile)],
+        lambda tile: beside(tile, jnp.logical_not(odd)),
+    )
+    for tile in range(count):
+        shade_ref[tile, last * 8 : last * 8 + 8] = final[tile]
 
 
 def picture_kernel(light_step, tiles, shade_ref, term_ref, clear_ref, pair_ref, *refs):
@@ -197,7 +230,7 @@
             out_ref[3, *at] = 1.0 - through
 
 
-def call(kernel, outs, ins, name, scratch=(), cost=1.0):
+def call(kernel, outs, ins, name, scratch=(), cost=1.0, aliases=None):
     cycles = int(cost * 1000)
     return pl.pallas_call(
         kernel,
@@ -207,6 +240,7 @@
         scratch_shapes=list(scratch),
         compiler_params=pltpu.CompilerParams(vmem_limit_bytes=8 * 2**20),
         cost_estimate=pl.CostEstimate(flops=cycles * 1000, bytes_accessed=cycles * 3000, transcendentals=0),
+        input_output_aliases=aliases or {},
         name=name,
     )(*ins)
 
@@ -248,7 +282,7 @@
     )(*[pltpu.with_memory_space_constraint(a, pltpu.HBM) for a in (density, bin_index, transfer, depth_order)])
 
     pair = lax.ppermute(send, "light", [(i, i ^ 1) for i in range(light_count)])
-    beside = [(i, i + 1) for i in range(1, light_count - 1, 2)]
+    beside = [(i, (i + 1) % light_count) for i in range(1, light_count, 2)]
     edge = lax.ppermute(edge, "light", beside + [(b, a) for a, b in beside])
     term, clear = call(
         functools.partial(terms_kernel, view_step),
@@ -256,7 +290,7 @@
         (table, entry, ext), "terms", cost=2.5,
     )
     shade = call(
-        functools.partial(shade_kernel, light_step), shape(*tiled), (dense, ext, pair, edge), "shade", cost=1.2
+        functools.partial(shade_kernel, light_step), shape(*tiled), (dense, ext), "shade", cost=1.2
     )
     group = send[0] + pair[0]
     groups = []
@@ -268,6 +302,10 @@
         groups.append(got)
         group = group + got
         step *= 2
+    shade = call(
+        functools.partial(outer_kernel, light_step, light_count), shape(*tiled),
+        (dense, ext, send, pair, edge, shade), "outer", cost=0.2, aliases={5: 0},
+    )
     pieces = call(
         functools.partial(picture_kernel, light_step, tile_count),
         [shape(4, light_cells, share)] * tile_count,

time: 31.2 us -> 27.5 us (0.88)
  the two profiles are of different devices: /device:TPU:11 before, /device:TPU:10 now
where the time goes in v3:
time: 27.5 us; the launch traced here: 27.3 us
  waiting for transfers between devices  12.4 us (45%)
  starting transfers between devices  7.89 us (29%)
  Pallas kernels  6.98 us (25%)
    ppermute x3, waiting for transfers between devices, per_device(): lax.ppermute(pieces[step], 'tile', [(i, (i + step) % tile_count) for i in...  8.27 us
    pallas_call x5, Pallas kernels, call(): pl.pallas_call(kernel, out_shape=outs, in_specs=[pl.BlockSpec(memory_spac...  4.71 us
    ppermute x3, starting transfers between devices, per_device(): lax.ppermute(pieces[step], 'tile', [(i, (i + step) % tile_count) for i in...  4.67 us
    ppermute x2, waiting for transfers between devices, per_device(): lax.ppermute(group, 'light', [(i, i ^ step) for i in range(light_count)])  2.76 us
    pallas_call x1, Pallas kernels, per_device(): pl.pallas_call(functools.partial(extinction_kernel, tile_count), out_shap...  2.27 us
    ppermute x2, starting transfers between devices, per_device(): lax.ppermute(group, 'light', [(i, i ^ step) for i in range(light_count)])  2.18 us
    ppermute x1, waiting for transfers between devices, per_device(): pair = lax.ppermute(send, 'light', [(i, i ^ 1) for i in range(light_count)])  1.33 us
    ppermute x1, starting transfers between devices, per_device(): edge = lax.ppermute(edge, 'light', beside + [(b, a) for a, b in beside])  0.96 us
  transfers between devices with their start and end apart: 7, of which 6 were waited for; matrix products, arithmetic and copies ran while one was open for 0% of the time, Pallas kernels for 12%

profile of v3, /device:TPU:10, one launch (start us, length us, event | category | flops | bytes accessed | tf_op | source)
XLA Modules:
  0.0 27.3 jit_solution(1435786019432932082)
XLA Ops:
  0.0 2.3 %extinction.1 = (f32[16,8,2048]{2,1,0:T(8,128)S(1)}, f32[4,128]{1,0:T(4,128)S(1)}, s32[16,128,128]{2,1,0:T(8,128)S(1)}, f32[16,128,128]{2,1,0:T(8,128)S(1)}, f32...) custom-call(f32[16,8,2048]{2,1,0:T(8,128)} %density_hbm.1, s32[16,8,2048]{2,1,0:T(8,128)} %bin_hbm.1, ...), custom_call_target="tpu_custom_call" | custom-call | tf_op jit(solution)/shard_map/extinction/pallas_call | solution.py:267
  2.3 0.1 collective-permute-start
  2.4 1.3 %collective-permute-done.pair_ref = f32[2,8,2048]{2,1,0:T(8,128)S(1)} collective-permute-done((f32[2,8,2048]{2,1,0:T(8,128)S(1)}, f32[2,8,2048]{2,1,0:T(8,128)S(1)}, u32[]{:S(2)}, u32[]{:S(2)}) %collective-permute-start) | collective-permute-done | bytes 131104 | tf_op jit(solution)/shard_map/ppermute | solution.py:284
  3.7 0.6 %collective-permute-start.2 = (f32[8,2048]{1,0:T(8,128)S(1)}, f32[8,2048]{1,0:T(8,128)S(1)}, u32[]{:S(2)}, u32[]{:S(2)}) collective-permute-start(f32[8,2048]{1,0:T(8,128)S(1)} %fusion), channel_id=1, source_target_pairs={{0,8},{4,12},{8,0},{12,4},{16,24},{20,28},{24,16},{28,20},{1,9},{5... | collective-permute-start | bytes 196616 | tf_op jit(solution)/shard_map/ppermute | solution.py:301
  4.3 1.0 %collective-permute-start.1 = (f32[8,2048]{1,0:T(8,128)S(1)}, f32[8,2048]{1,0:T(8,128)S(1)}, u32[]{:S(2)}, u32[]{:S(2)}) collective-permute-start(f32[8,2048]{1,0:T(8,128)S(1)} %get-tuple-element.24), channel_id=1, source_target_pairs={{4,8},{12,16},{20,24},{28,0},{8,4},{16,12},{24,20},{0,28},{5,9},{1... | collective-permute-start | bytes 196616 | tf_op jit(solution)/shard_map/ppermute | solution.py:286
  5.3 1.1 %shade.1._ = f32[16,128,128]{2,1,0:T(8,128)S(1)} custom-call(f32[16,8,2048]{2,1,0:T(8,128)S(1)} %get-tuple-element.21.density_ref, f32[16,128,128]{2,1,0:T(8,128)S(1)} %get-tuple-element.22.ext_ref), custom_call_target="tpu_custom_call" | custom-call | flops 1200000 | bytes 3600000 | tf_op jit(solution)/shard_map/shade/pallas_call | solution.py:235
  6.4 2.3 %collective-permute-done.2.refs_0_ = f32[8,2048]{1,0:T(8,128)S(1)} collective-permute-done((f32[8,2048]{1,0:T(8,128)S(1)}, f32[8,2048]{1,0:T(8,128)S(1)}, u32[]{:S(2)}, u32[]{:S(2)}) %collective-permute-start.2) | collective-permute-done | bytes 65568 | tf_op jit(solution)/shard_map/ppermute | solution.py:301
  8.7 1.6 %collective-permute-start.3 = (f32[8,2048]{1,0:T(8,128)S(1)}, f32[8,2048]{1,0:T(8,128)S(1)}, u32[]{:S(2)}, u32[]{:S(2)}) collective-permute-start(f32[8,2048]{1,0:T(8,128)S(1)} %add.11), channel_id=1, source_target_pairs={{0,16},{4,20},{8,24},{12,28},{16,0},{20,4},{24,8},{28,12},{1,17},{... | collective-permute-start | bytes 196616 | tf_op jit(solution)/shard_map/ppermute | solution.py:301
  10.3 2.2 %terms.1 = (f32[3,8,16,2048]{3,2,1,0:T(8,128)S(1)}, f32[16,2048]{1,0:T(8,128)S(1)}) custom-call(f32[4,128]{1,0:T(4,128)S(1)} %get-tuple-element.26.table_ref, s32[16,128,128]{2,1,0:T(8,128)S(1)} %get-tuple-element.27.entry_ref, f32[16,128,128]{2,1,0:T(8,128)S(1)} %get-tuple-element.22.ext_ref), custom_call_target="tpu_custom_call" | custom-call | flops 2500000 | bytes 7500000 | tf_op jit(solution)/shard_map/terms/pallas_call | solution.py:235
  12.5 0.0 collective-permute-done.1.edge_ref
  12.5 0.1 outer.1.shade_ref
  12.6 0.4 %collective-permute-done.3.refs_1_ = f32[8,2048]{1,0:T(8,128)S(1)} collective-permute-done((f32[8,2048]{1,0:T(8,128)S(1)}, f32[8,2048]{1,0:T(8,128)S(1)}, u32[]{:S(2)}, u32[]{:S(2)}) %collective-permute-start.3) | collective-permute-done | bytes 65568 | tf_op jit(solution)/shard_map/ppermute | solution.py:301
  13.0 0.6 %picture.1 = (f32[4,16,512]{2,1,0:T(8,128)S(1)}, f32[4,16,512]{2,1,0:T(8,128)S(1)}, f32[4,16,512]{2,1,0:T(8,128)S(1)}, f32[4,16,512]{2,1,0:T(8,128)S(1)}) custom-call(f32[16,128,128]{2,1,0:T(8,128)S(1)} %outer.1.shade_ref, f32[3,8,16,2048]{3,2,1,0:T(8,128)S(1)} %get-tuple-element.28.term_ref, f32[16,2048]{1,0:T(8,128)S(1)} %get-tuple-element.29.clear_ref, ...), custom_call_target="tpu_custom_call" | custom-call | flops 600000 | bytes 1800000 | tf_op jit(solution)/shard_map/picture/pallas_call | solution.py:235
  13.7 1.6 %collective-permute-start.4 = (f32[4,16,512]{2,1,0:T(8,128)S(1)}, f32[4,16,512]{2,1,0:T(8,128)S(1)}, u32[]{:S(2)}, u32[]{:S(2)}) collective-permute-start(f32[4,16,512]{2,1,0:T(8,128)S(1)} %get-tuple-element.32), channel_id=1, source_target_pairs={{0,1},{1,2},{2,3},{3,0},{4,5},{5,6},{6,7},{7,4},{8,9},{9,10},{10,1... | collective-permute-start | bytes 393224 | tf_op jit(solution)/shard_map/ppermute | solution.py:318
  15.3 1.2 %collective-permute-start.5 = (f32[4,16,512]{2,1,0:T(8,128)S(1)}, f32[4,16,512]{2,1,0:T(8,128)S(1)}, u32[]{:S(2)}, u32[]{:S(2)}) collective-permute-start(f32[4,16,512]{2,1,0:T(8,128)S(1)} %get-tuple-element.33), channel_id=1, source_target_pairs={{0,2},{1,3},{2,0},{3,1},{4,6},{5,7},{6,4},{7,5},{8,10},{9,11},{10,... | collective-permute-start | bytes 393224 | tf_op jit(solution)/shard_map/ppermute | solution.py:318
  16.4 1.9 %collective-permute-start.6 = (f32[4,16,512]{2,1,0:T(8,128)S(1)}, f32[4,16,512]{2,1,0:T(8,128)S(1)}, u32[]{:S(2)}, u32[]{:S(2)}) collective-permute-start(f32[4,16,512]{2,1,0:T(8,128)S(1)} %get-tuple-element.34), channel_id=1, source_target_pairs={{0,3},{1,0},{2,1},{3,2},{4,7},{5,4},{6,5},{7,6},{8,11},{9,8},{10,9... | collective-permute-start | bytes 393224 | tf_op jit(solution)/shard_map/ppermute | solution.py:318
  18.3 5.1 %collective-permute-done.4.refs_1_ = f32[4,16,512]{2,1,0:T(8,128)S(1)} collective-permute-done((f32[4,16,512]{2,1,0:T(8,128)S(1)}, f32[4,16,512]{2,1,0:T(8,128)S(1)}, u32[]{:S(2)}, u32[]{:S(2)}) %collective-permute-start.4) | collective-permute-done | bytes 131104 | tf_op jit(solution)/shard_map/ppermute | solution.py:318
  23.4 1.4 %collective-permute-done.5.refs_2_ = f32[4,16,512]{2,1,0:T(8,128)S(1)} collective-permute-done((f32[4,16,512]{2,1,0:T(8,128)S(1)}, f32[4,16,512]{2,1,0:T(8,128)S(1)}, u32[]{:S(2)}, u32[]{:S(2)}) %collective-permute-start.5) | collective-permute-done | bytes 131104 | tf_op jit(solution)/shard_map/ppermute | solution.py:318
  24.8 1.8 %collective-permute-done.6.refs_3_ = f32[4,16,512]{2,1,0:T(8,128)S(1)} collective-permute-done((f32[4,16,512]{2,1,0:T(8,128)S(1)}, f32[4,16,512]{2,1,0:T(8,128)S(1)}, u32[]{:S(2)}, u32[]{:S(2)}) %collective-permute-start.6) | collective-permute-done | bytes 131104 | tf_op jit(solution)/shard_map/ppermute | solution.py:318
  26.6 0.7 %combine.1 = f32[4,16,512]{2,1,0:T(8,128)} custom-call(f32[16,8,128]{2,1,0:T(8,128)S(1)} %get-tuple-element.20.front_ref, f32[4,16,512]{2,1,0:T(8,128)S(1)} %get-tuple-element.31.refs_0_, f32[4,16,512]{2,1,0:T(8,128)S(1)} %collective-permute-done.4.refs_1_, f32[4,16,512]{2,1,0:T(8,128)S(1)} %collective-permute-done.5.refs_2_, ...), custom_call_target="tpu_custom_call" | custom-call | flops 1000000 | bytes 3000000 | tf_op jit(solution)/shard_map/combine/pallas_call | solution.py:235
  (2 shorter events, 0.0 us)
Async XLA Ops:
  2.3 1.4 %collective-permute-start = (f32[2,8,2048]{2,1,0:T(8,128)S(1)}, f32[2,8,2048]{2,1,0:T(8,128)S(1)}, u32[]{:S(2)}, u32[]{:S(2)}) collective-permute-start(f32[2,8,2048]{2,1,0:T(8,128)S(1)} %get-tuple-element.23.send_ref), channel_id=1, source_target_pairs={{0,4},{4,0},{8,12},{12,8},{16,20},{20,16},{24,28},{28,24},{1,5},{5... | collective-permute-start | bytes 393224 | tf_op jit(solution)/shard_map/ppermute | solution.py:284
  3.7 5.0 %collective-permute-start.2 = (f32[8,2048]{1,0:T(8,128)S(1)}, f32[8,2048]{1,0:T(8,128)S(1)}, u32[]{:S(2)}, u32[]{:S(2)}) collective-permute-start(f32[8,2048]{1,0:T(8,128)S(1)} %fusion), channel_id=1, source_target_pairs={{0,8},{4,12},{8,0},{12,4},{16,24},{20,28},{24,16},{28,20},{1,9},{5... | collective-permute-start | bytes 196616 | tf_op jit(solution)/shard_map/ppermute | solution.py:301
  4.3 8.2 %collective-permute-start.1 = (f32[8,2048]{1,0:T(8,128)S(1)}, f32[8,2048]{1,0:T(8,128)S(1)}, u32[]{:S(2)}, u32[]{:S(2)}) collective-permute-start(f32[8,2048]{1,0:T(8,128)S(1)} %get-tuple-element.24), channel_id=1, source_target_pairs={{4,8},{12,16},{20,24},{28,0},{8,4},{16,12},{24,20},{0,28},{5,9},{1... | collective-permute-start | bytes 196616 | tf_op jit(solution)/shard_map/ppermute | solution.py:286
  8.7 4.3 %collective-permute-start.3 = (f32[8,2048]{1,0:T(8,128)S(1)}, f32[8,2048]{1,0:T(8,128)S(1)}, u32[]{:S(2)}, u32[]{:S(2)}) collective-permute-start(f32[8,2048]{1,0:T(8,128)S(1)} %add.11), channel_id=1, source_target_pairs={{0,16},{4,20},{8,24},{12,28},{16,0},{20,4},{24,8},{28,12},{1,17},{... | collective-permute-start | bytes 196616 | tf_op jit(solution)/shard_map/ppermute | solution.py:301
  13.7 9.7 %collective-permute-start.4 = (f32[4,16,512]{2,1,0:T(8,128)S(1)}, f32[4,16,512]{2,1,0:T(8,128)S(1)}, u32[]{:S(2)}, u32[]{:S(2)}) collective-permute-start(f32[4,16,512]{2,1,0:T(8,128)S(1)} %get-tuple-element.32), channel_id=1, source_target_pairs={{0,1},{1,2},{2,3},{3,0},{4,5},{5,6},{6,7},{7,4},{8,9},{9,10},{10,1... | collective-permute-start | bytes 393224 | tf_op jit(solution)/shard_map/ppermute | solution.py:318
  15.3 9.5 %collective-permute-start.5 = (f32[4,16,512]{2,1,0:T(8,128)S(1)}, f32[4,16,512]{2,1,0:T(8,128)S(1)}, u32[]{:S(2)}, u32[]{:S(2)}) collective-permute-start(f32[4,16,512]{2,1,0:T(8,128)S(1)} %get-tuple-element.33), channel_id=1, source_target_pairs={{0,2},{1,3},{2,0},{3,1},{4,6},{5,7},{6,4},{7,5},{8,10},{9,11},{10,... | collective-permute-start | bytes 393224 | tf_op jit(solution)/shard_map/ppermute | solution.py:318
  16.4 10.2 %collective-permute-start.6 = (f32[4,16,512]{2,1,0:T(8,128)S(1)}, f32[4,16,512]{2,1,0:T(8,128)S(1)}, u32[]{:S(2)}, u32[]{:S(2)}) collective-permute-start(f32[4,16,512]{2,1,0:T(8,128)S(1)} %get-tuple-element.34), channel_id=1, source_target_pairs={{0,3},{1,0},{2,1},{3,2},{4,7},{5,4},{6,5},{7,6},{8,11},{9,8},{10,9... | collective-permute-start | bytes 393224 | tf_op jit(solution)/shard_map/ppermute | solution.py:318

commit v4 on v3

--- a/solution.py
+++ b/solution.py
@@ -94,7 +94,7 @@
     _, depth_cells, light_cells, columns = term_ref.shape
     tables = [table_rows(table_ref, c) for c in range(3)]
 
-    @pl.loop(0, columns // LANES, unroll=2)
+    @pl.loop(0, columns // LANES, unroll=4)
     def _(tile):
         at = pl.ds(pl.multiple_of(tile * LANES, LANES), LANES)
         for half in range(0, light_cells, 8):
@@ -178,15 +178,15 @@
         shade_ref[tile, last * 8 : last * 8 + 8] = final[tile]
 
 
-def picture_kernel(light_step, tiles, shade_ref, term_ref, clear_ref, pair_ref, *refs):
+def picture_kernel(light_step, tiles, masks, shade_ref, term_ref, clear_ref, pair_ref, *refs):
     group_refs, out_refs, fade_ref = refs[: -tiles - 1], refs[-tiles - 1 : -1], refs[-1]
     _, depth_cells, light_cells, columns = term_ref.shape
     share = columns // tiles
     mine = lax.axis_index("tile")
     place = lax.axis_index("light")
     upstream = jnp.where((place & 1) > 0, pair_ref[0], 0.0)
-    for level, group_ref in enumerate(group_refs):
-        upstream = upstream + jnp.where((place & (2 << level)) > 0, group_ref[...], 0.0)
+    for mask, group_ref in zip(masks, group_refs):
+        upstream = upstream + jnp.where((place ^ mask) < place, group_ref[...], 0.0)
     fade_ref[...] = jnp.exp2(upstream * (-light_step * LOG2E))
     for step, out_ref in enumerate(out_refs):
         owner = lax.rem(mine + step, tiles)
@@ -294,20 +294,21 @@
     )
     group = send[0] + pair[0]
     groups = []
+    masks = []
     step = 2
     while step < light_count:
-        if step == light_count // 2:
-            group, shade = lax.optimization_barrier((group, shade))
-        got = lax.ppermute(group, "light", [(i, i ^ step) for i in range(light_count)])
-        groups.append(got)
-        group = group + got
-        step *= 2
+        reach = [m * step for m in (1, 2, 3)] if step * 4 <= light_count else [step]
+        got = [lax.ppermute(group, "light", [(i, i ^ m) for i in range(light_count)]) for m in reach]
+        groups += got
+        masks += reach
+        group = group + functools.reduce(jnp.add, got)
+        step *= len(reach) + 1
     shade = call(
         functools.partial(outer_kernel, light_step, light_count), shape(*tiled),
         (dense, ext, send, pair, edge, shade), "outer", cost=0.2, aliases={5: 0},
     )
     pieces = call(
-        functools.partial(picture_kernel, light_step, tile_count),
+        functools.partial(picture_kernel, light_step, tile_count, masks),
         [shape(4, light_cells, share)] * tile_count,
         (shade, term, clear, pair, *groups), "picture",
         scratch=[pltpu.VMEM(plane.shape, F32)], cost=0.6,

time: 27.5 us -> 26.9 us (0.978)
  the two profiles are of different devices: /device:TPU:10 before, /device:TPU:0 now
where the time goes in v4:
time: 26.9 us; the launch traced here: 26.3 us
  starting transfers between devices  13.2 us (49%)
  Pallas kernels  6.71 us (25%)
  waiting for transfers between devices  6.36 us (24%)
    ppermute x3, waiting for transfers between devices, per_device(): lax.ppermute(pieces[step], 'tile', [(i, (i + step) % tile_count) for i in...  6.05 us
    ppermute x3, starting transfers between devices, per_device(): lax.ppermute(pieces[step], 'tile', [(i, (i + step) % tile_count) for i in...  5.57 us
    pallas_call x5, Pallas kernels, call(): pl.pallas_call(kernel, out_shape=outs, in_specs=[pl.BlockSpec(memory_spac...  4.44 us
    ppermute x1, starting transfers between devices, per_device(): edge = lax.ppermute(edge, 'light', beside + [(b, a) for a, b in beside])  3.56 us
    ppermute x3, starting transfers between devices, per_device(): lax.ppermute(group, 'light', [(i, i ^ m) for i in range(light_count)])  3.55 us
    pallas_call x1, Pallas kernels, per_device(): pl.pallas_call(functools.partial(extinction_kernel, tile_count), out_shap...  2.27 us
  transfers between devices with their start and end apart: 8, of which 4 were waited for; matrix products, arithmetic and copies ran while one was open for 0% of the time, Pallas kernels for 12%

profile of v4, /device:TPU:0, one launch (start us, length us, event | category | flops | bytes accessed | tf_op | source)
XLA Modules:
  0.0 26.3 jit_solution(12828244049328800)
XLA Ops:
  0.0 2.3 %extinction.1 = (f32[16,8,2048]{2,1,0:T(8,128)S(1)}, f32[4,128]{1,0:T(4,128)S(1)}, s32[16,128,128]{2,1,0:T(8,128)S(1)}, f32[16,128,128]{2,1,0:T(8,128)S(1)}, f32...) custom-call(f32[16,8,2048]{2,1,0:T(8,128)} %density_hbm.1, s32[16,8,2048]{2,1,0:T(8,128)} %bin_hbm.1, ...), custom_call_target="tpu_custom_call" | custom-call | tf_op jit(solution)/shard_map/extinction/pallas_call | solution.py:267
  2.3 0.5 %collective-permute-start = (f32[2,8,2048]{2,1,0:T(8,128)S(1)}, f32[2,8,2048]{2,1,0:T(8,128)S(1)}, u32[]{:S(2)}, u32[]{:S(2)}) collective-permute-start(f32[2,8,2048]{2,1,0:T(8,128)S(1)} %get-tuple-element.21.send_ref), channel_id=1, source_target_pairs={{0,4},{4,0},{8,12},{12,8},{16,20},{20,16},{24,28},{28,24},{1,5},{5... | collective-permute-start | bytes 393224 | tf_op jit(solution)/shard_map/ppermute | solution.py:284
  2.8 3.6 %collective-permute-start.1 = (f32[8,2048]{1,0:T(8,128)S(1)}, f32[8,2048]{1,0:T(8,128)S(1)}, u32[]{:S(2)}, u32[]{:S(2)}) collective-permute-start(f32[8,2048]{1,0:T(8,128)S(1)} %get-tuple-element.22), channel_id=1, source_target_pairs={{4,8},{12,16},{20,24},{28,0},{8,4},{16,12},{24,20},{0,28},{5,9},{1... | collective-permute-start | bytes 196616 | tf_op jit(solution)/shard_map/ppermute | solution.py:286
  6.4 0.0 collective-permute-done.pair_ref
  6.4 0.3 %collective-permute-start.2 = (f32[8,2048]{1,0:T(8,128)S(1)}, f32[8,2048]{1,0:T(8,128)S(1)}, u32[]{:S(2)}, u32[]{:S(2)}) collective-permute-start(f32[8,2048]{1,0:T(8,128)S(1)} %fusion), channel_id=1, source_target_pairs={{0,8},{4,12},{8,0},{12,4},{16,24},{20,28},{24,16},{28,20},{1,9},{5... | collective-permute-start | bytes 196616 | tf_op jit(solution)/shard_map/ppermute | solution.py:301
  6.7 1.5 %collective-permute-start.3 = (f32[8,2048]{1,0:T(8,128)S(1)}, f32[8,2048]{1,0:T(8,128)S(1)}, u32[]{:S(2)}, u32[]{:S(2)}) collective-permute-start(f32[8,2048]{1,0:T(8,128)S(1)} %fusion), channel_id=1, source_target_pairs={{0,16},{4,20},{8,24},{12,28},{16,0},{20,4},{24,8},{28,12},{1,17},{... | collective-permute-start | bytes 196616 | tf_op jit(solution)/shard_map/ppermute | solution.py:301
  8.2 1.7 %collective-permute-start.4 = (f32[8,2048]{1,0:T(8,128)S(1)}, f32[8,2048]{1,0:T(8,128)S(1)}, u32[]{:S(2)}, u32[]{:S(2)}) collective-permute-start(f32[8,2048]{1,0:T(8,128)S(1)} %fusion), channel_id=1, source_target_pairs={{0,24},{4,28},{8,16},{12,20},{16,8},{20,12},{24,0},{28,4},{1,25},{... | collective-permute-start | bytes 196616 | tf_op jit(solution)/shard_map/ppermute | solution.py:301
  9.9 1.1 %shade.1._ = f32[16,128,128]{2,1,0:T(8,128)S(1)} custom-call(f32[16,8,2048]{2,1,0:T(8,128)S(1)} %get-tuple-element.19.density_ref, f32[16,128,128]{2,1,0:T(8,128)S(1)} %get-tuple-element.20.ext_ref), custom_call_target="tpu_custom_call" | custom-call | flops 1200000 | bytes 3600000 | tf_op jit(solution)/shard_map/shade/pallas_call | solution.py:235
  11.0 1.9 %terms.1 = (f32[3,8,16,2048]{3,2,1,0:T(8,128)S(1)}, f32[16,2048]{1,0:T(8,128)S(1)}) custom-call(f32[4,128]{1,0:T(4,128)S(1)} %get-tuple-element.23.table_ref, s32[16,128,128]{2,1,0:T(8,128)S(1)} %get-tuple-element.24.entry_ref, f32[16,128,128]{2,1,0:T(8,128)S(1)} %get-tuple-element.20.ext_ref), custom_call_target="tpu_custom_call" | custom-call | flops 2500000 | bytes 7500000 | tf_op jit(solution)/shard_map/terms/pallas_call | solution.py:235
  12.9 0.0 collective-permute-done.1.edge_ref
  12.9 0.1 outer.1.shade_ref
  13.1 0.0 collective-permute-done.2.refs_0_
  13.1 0.0 collective-permute-done.3.refs_1_
  13.1 0.3 %collective-permute-done.4.refs_2_ = f32[8,2048]{1,0:T(8,128)S(1)} collective-permute-done((f32[8,2048]{1,0:T(8,128)S(1)}, f32[8,2048]{1,0:T(8,128)S(1)}, u32[]{:S(2)}, u32[]{:S(2)}) %collective-permute-start.4) | collective-permute-done | bytes 65568 | tf_op jit(solution)/shard_map/ppermute | solution.py:301
  13.4 0.6 %picture.1 = (f32[4,16,512]{2,1,0:T(8,128)S(1)}, f32[4,16,512]{2,1,0:T(8,128)S(1)}, f32[4,16,512]{2,1,0:T(8,128)S(1)}, f32[4,16,512]{2,1,0:T(8,128)S(1)}) custom-call(f32[16,128,128]{2,1,0:T(8,128)S(1)} %outer.1.shade_ref, f32[3,8,16,2048]{3,2,1,0:T(8,128)S(1)} %get-tuple-element.25.term_ref, f32[16,2048]{1,0:T(8,128)S(1)} %get-tuple-element.26.clear_ref, ...), custom_call_target="tpu_custom_call" | custom-call | flops 600000 | bytes 1800000 | tf_op jit(solution)/shard_map/picture/pallas_call | solution.py:235
  14.0 1.6 %collective-permute-start.5 = (f32[4,16,512]{2,1,0:T(8,128)S(1)}, f32[4,16,512]{2,1,0:T(8,128)S(1)}, u32[]{:S(2)}, u32[]{:S(2)}) collective-permute-start(f32[4,16,512]{2,1,0:T(8,128)S(1)} %get-tuple-element.28), channel_id=1, source_target_pairs={{0,1},{1,2},{2,3},{3,0},{4,5},{5,6},{6,7},{7,4},{8,9},{9,10},{10,1... | collective-permute-start | bytes 393224 | tf_op jit(solution)/shard_map/ppermute | solution.py:319
  15.6 2.6 %collective-permute-start.6 = (f32[4,16,512]{2,1,0:T(8,128)S(1)}, f32[4,16,512]{2,1,0:T(8,128)S(1)}, u32[]{:S(2)}, u32[]{:S(2)}) collective-permute-start(f32[4,16,512]{2,1,0:T(8,128)S(1)} %get-tuple-element.29), channel_id=1, source_target_pairs={{0,2},{1,3},{2,0},{3,1},{4,6},{5,7},{6,4},{7,5},{8,10},{9,11},{10,... | collective-permute-start | bytes 393224 | tf_op jit(solution)/shard_map/ppermute | solution.py:319
  18.2 1.3 %collective-permute-start.7 = (f32[4,16,512]{2,1,0:T(8,128)S(1)}, f32[4,16,512]{2,1,0:T(8,128)S(1)}, u32[]{:S(2)}, u32[]{:S(2)}) collective-permute-start(f32[4,16,512]{2,1,0:T(8,128)S(1)} %get-tuple-element.30), channel_id=1, source_target_pairs={{0,3},{1,0},{2,1},{3,2},{4,7},{5,4},{6,5},{7,6},{8,11},{9,8},{10,9... | collective-permute-start | bytes 393224 | tf_op jit(solution)/shard_map/ppermute | solution.py:319
  19.6 2.8 %collective-permute-done.5.refs_1_ = f32[4,16,512]{2,1,0:T(8,128)S(1)} collective-permute-done((f32[4,16,512]{2,1,0:T(8,128)S(1)}, f32[4,16,512]{2,1,0:T(8,128)S(1)}, u32[]{:S(2)}, u32[]{:S(2)}) %collective-permute-start.5) | collective-permute-done | bytes 131104 | tf_op jit(solution)/shard_map/ppermute | solution.py:319
  22.4 3.2 %collective-permute-done.6.refs_2_ = f32[4,16,512]{2,1,0:T(8,128)S(1)} collective-permute-done((f32[4,16,512]{2,1,0:T(8,128)S(1)}, f32[4,16,512]{2,1,0:T(8,128)S(1)}, u32[]{:S(2)}, u32[]{:S(2)}) %collective-permute-start.6) | collective-permute-done | bytes 131104 | tf_op jit(solution)/shard_map/ppermute | solution.py:319
  25.6 0.1 collective-permute-done.7.refs_3_
  25.6 0.7 %combine.1 = f32[4,16,512]{2,1,0:T(8,128)} custom-call(f32[16,8,128]{2,1,0:T(8,128)S(1)} %get-tuple-element.18.front_ref, f32[4,16,512]{2,1,0:T(8,128)S(1)} %get-tuple-element.27.refs_0_, f32[4,16,512]{2,1,0:T(8,128)S(1)} %collective-permute-done.5.refs_1_, f32[4,16,512]{2,1,0:T(8,128)S(1)} %collective-permute-done.6.refs_2_, ...), custom_call_target="tpu_custom_call" | custom-call | flops 1000000 | bytes 3000000 | tf_op jit(solution)/shard_map/combine/pallas_call | solution.py:235
  (1 shorter events, 0.0 us)
Async XLA Ops:
  2.3 4.1 %collective-permute-start = (f32[2,8,2048]{2,1,0:T(8,128)S(1)}, f32[2,8,2048]{2,1,0:T(8,128)S(1)}, u32[]{:S(2)}, u32[]{:S(2)}) collective-permute-start(f32[2,8,2048]{2,1,0:T(8,128)S(1)} %get-tuple-element.21.send_ref), channel_id=1, source_target_pairs={{0,4},{4,0},{8,12},{12,8},{16,20},{20,16},{24,28},{28,24},{1,5},{5... | collective-permute-start | bytes 393224 | tf_op jit(solution)/shard_map/ppermute | solution.py:284
  2.8 10.1 %collective-permute-start.1 = (f32[8,2048]{1,0:T(8,128)S(1)}, f32[8,2048]{1,0:T(8,128)S(1)}, u32[]{:S(2)}, u32[]{:S(2)}) collective-permute-start(f32[8,2048]{1,0:T(8,128)S(1)} %get-tuple-element.22), channel_id=1, source_target_pairs={{4,8},{12,16},{20,24},{28,0},{8,4},{16,12},{24,20},{0,28},{5,9},{1... | collective-permute-start | bytes 196616 | tf_op jit(solution)/shard_map/ppermute | solution.py:286
  6.4 6.7 %collective-permute-start.2 = (f32[8,2048]{1,0:T(8,128)S(1)}, f32[8,2048]{1,0:T(8,128)S(1)}, u32[]{:S(2)}, u32[]{:S(2)}) collective-permute-start(f32[8,2048]{1,0:T(8,128)S(1)} %fusion), channel_id=1, source_target_pairs={{0,8},{4,12},{8,0},{12,4},{16,24},{20,28},{24,16},{28,20},{1,9},{5... | collective-permute-start | bytes 196616 | tf_op jit(solution)/shard_map/ppermute | solution.py:301
  6.7 6.4 %collective-permute-start.3 = (f32[8,2048]{1,0:T(8,128)S(1)}, f32[8,2048]{1,0:T(8,128)S(1)}, u32[]{:S(2)}, u32[]{:S(2)}) collective-permute-start(f32[8,2048]{1,0:T(8,128)S(1)} %fusion), channel_id=1, source_target_pairs={{0,16},{4,20},{8,24},{12,28},{16,0},{20,4},{24,8},{28,12},{1,17},{... | collective-permute-start | bytes 196616 | tf_op jit(solution)/shard_map/ppermute | solution.py:301
  8.2 5.2 %collective-permute-start.4 = (f32[8,2048]{1,0:T(8,128)S(1)}, f32[8,2048]{1,0:T(8,128)S(1)}, u32[]{:S(2)}, u32[]{:S(2)}) collective-permute-start(f32[8,2048]{1,0:T(8,128)S(1)} %fusion), channel_id=1, source_target_pairs={{0,24},{4,28},{8,16},{12,20},{16,8},{20,12},{24,0},{28,4},{1,25},{... | collective-permute-start | bytes 196616 | tf_op jit(solution)/shard_map/ppermute | solution.py:301
  14.0 8.3 %collective-permute-start.5 = (f32[4,16,512]{2,1,0:T(8,128)S(1)}, f32[4,16,512]{2,1,0:T(8,128)S(1)}, u32[]{:S(2)}, u32[]{:S(2)}) collective-permute-start(f32[4,16,512]{2,1,0:T(8,128)S(1)} %get-tuple-element.28), channel_id=1, source_target_pairs={{0,1},{1,2},{2,3},{3,0},{4,5},{5,6},{6,7},{7,4},{8,9},{9,10},{10,1... | collective-permute-start | bytes 393224 | tf_op jit(solution)/shard_map/ppermute | solution.py:319
  15.6 9.9 %collective-permute-start.6 = (f32[4,16,512]{2,1,0:T(8,128)S(1)}, f32[4,16,512]{2,1,0:T(8,128)S(1)}, u32[]{:S(2)}, u32[]{:S(2)}) collective-permute-start(f32[4,16,512]{2,1,0:T(8,128)S(1)} %get-tuple-element.29), channel_id=1, source_target_pairs={{0,2},{1,3},{2,0},{3,1},{4,6},{5,7},{6,4},{7,5},{8,10},{9,11},{10,... | collective-permute-start | bytes 393224 | tf_op jit(solution)/shard_map/ppermute | solution.py:319
  18.2 7.4 %collective-permute-start.7 = (f32[4,16,512]{2,1,0:T(8,128)S(1)}, f32[4,16,512]{2,1,0:T(8,128)S(1)}, u32[]{:S(2)}, u32[]{:S(2)}) collective-permute-start(f32[4,16,512]{2,1,0:T(8,128)S(1)} %get-tuple-element.30), channel_id=1, source_target_pairs={{0,3},{1,0},{2,1},{3,2},{4,7},{5,4},{6,5},{7,6},{8,11},{9,8},{10,9... | collective-permute-start | bytes 393224 | tf_op jit(solution)/shard_map/ppermute | solution.py:319

commit v5 on v4

--- a/solution.py
+++ b/solution.py
@@ -82,7 +82,7 @@
     for part, (first, second) in enumerate(copies):
         first.wait()
         second.wait()
-        running = lax.fori_loop(part * size, (part + 1) * size, layer, running, unroll=min(4, size))
+        running = lax.fori_loop(part * size, (part + 1) * size, layer, running, unroll=size)
     for tile in range(tiles):
         send_ref[0, :, lanes(tile)] = running[tile]
     odd = lax.rem(lax.axis_index("light"), 2)
@@ -178,8 +178,8 @@
         shade_ref[tile, last * 8 : last * 8 + 8] = final[tile]
 
 
-def picture_kernel(light_step, tiles, masks, shade_ref, term_ref, clear_ref, pair_ref, *refs):
-    group_refs, out_refs, fade_ref = refs[: -tiles - 1], refs[-tiles - 1 : -1], refs[-1]
+def picture_kernel(light_step, tiles, masks, steps, shade_ref, term_ref, clear_ref, pair_ref, *refs):
+    group_refs, out_refs, fade_ref = refs[: -len(steps) - 1], refs[-len(steps) - 1 : -1], refs[-1]
     _, depth_cells, light_cells, columns = term_ref.shape
     share = columns // tiles
     mine = lax.axis_index("tile")
@@ -188,7 +188,7 @@
     for mask, group_ref in zip(masks, group_refs):
         upstream = upstream + jnp.where((place ^ mask) < place, group_ref[...], 0.0)
     fade_ref[...] = jnp.exp2(upstream * (-light_step * LOG2E))
-    for step, out_ref in enumerate(out_refs):
+    for step, out_ref in zip(steps, out_refs):
         owner = lax.rem(mine + step, tiles)
         for tile in range(share // LANES):
             at = pl.ds(pl.multiple_of(owner * share + tile * LANES, LANES), LANES)
@@ -307,18 +307,21 @@
         functools.partial(outer_kernel, light_step, light_count), shape(*tiled),
         (dense, ext, send, pair, edge, shade), "outer", cost=0.2, aliases={5: 0},
     )
-    pieces = call(
-        functools.partial(picture_kernel, light_step, tile_count, masks),
-        [shape(4, light_cells, share)] * tile_count,
-        (shade, term, clear, pair, *groups), "picture",
-        scratch=[pltpu.VMEM(plane.shape, F32)], cost=0.6,
-    )
-    held = [pieces[0]]
-    for step in range(1, tile_count):
-        held.append(
-            lax.ppermute(pieces[step], "tile", [(i, (i + step) % tile_count) for i in range(tile_count)])
+    held = {}
+    for steps in ([1], [*range(2, tile_count), 0]):
+        pieces = call(
+            functools.partial(picture_kernel, light_step, tile_count, masks, steps),
+            [shape(4, light_cells, share)] * len(steps),
+            (shade, term, clear, pair, *groups), "picture",
+            scratch=[pltpu.VMEM(plane.shape, F32)], cost=0.2 * len(steps),
         )
-    return call(combine_kernel, shape(4, light_cells, share), (front, *held), "combine")
+        for step, piece in zip(steps, pieces):
+            held[step] = piece
+            if step:
+                held[step] = lax.ppermute(piece, "tile", [(i, (i + step) % tile_count) for i in range(tile_count)])
+    return call(
+        combine_kernel, shape(4, light_cells, share), (front, *[held[step] for step in range(tile_count)]), "combine"
+    )
 
 
 def solution(mesh):

time: 26.9 us -> 26.2 us (0.974); the launches traced: 26.3 us -> 26.1 us
    pallas_call x5 -> x6, Pallas kernels: 4.44 us -> 4.47 us  [call(): pl.pallas_call(kernel, out_shape=outs, in_specs=[pl.BlockSpec(memory_spac...]
  transfers between devices with their start and end apart: 8 -> 8, of which waited for: 4 -> 3; matrix products, arithmetic and copies ran while one was open for 0% -> 0% of each run, Pallas kernels for 12% -> 14%
where the time goes in v5:
time: 26.2 us; the launch traced here: 26.1 us
  starting transfers between devices  13.3 us (51%)
  Pallas kernels  6.59 us (25%)
  waiting for transfers between devices  6.13 us (23%)
    ppermute x3, waiting for transfers between devices, per_device(): lax.ppermute(piece, 'tile', [(i, (i + step) % tile_count) for i in range(...  5.81 us
    ppermute x3, starting transfers between devices, per_device(): lax.ppermute(piece, 'tile', [(i, (i + step) % tile_count) for i in range(...  5.63 us
    pallas_call x6, Pallas kernels, call(): pl.pallas_call(kernel, out_shape=outs, in_specs=[pl.BlockSpec(memory_spac...  4.47 us
    ppermute x1, starting transfers between devices, per_device(): edge = lax.ppermute(edge, 'light', beside + [(b, a) for a, b in beside])  3.56 us
    ppermute x3, starting transfers between devices, per_device(): lax.ppermute(group, 'light', [(i, i ^ m) for i in range(light_count)])  3.55 us
    pallas_call x1, Pallas kernels, per_device(): pl.pallas_call(functools.partial(extinction_kernel, tile_count), out_shap...  2.13 us
  transfers between devices with their start and end apart: 8, of which 3 were waited for; matrix products, arithmetic and copies ran while one was open for 0% of the time, Pallas kernels for 14%

profile of v5, /device:TPU:0, one launch (start us, length us, event | category | flops | bytes accessed | tf_op | source)
XLA Modules:
  0.0 26.1 jit_solution(9025531185617988491)
XLA Ops:
  0.0 2.1 %extinction.1 = (f32[16,8,2048]{2,1,0:T(8,128)S(1)}, f32[4,128]{1,0:T(4,128)S(1)}, s32[16,128,128]{2,1,0:T(8,128)S(1)}, f32[16,128,128]{2,1,0:T(8,128)S(1)}, f32...) custom-call(f32[16,8,2048]{2,1,0:T(8,128)} %density_hbm.1, s32[16,8,2048]{2,1,0:T(8,128)} %bin_hbm.1, ...), custom_call_target="tpu_custom_call" | custom-call | tf_op jit(solution)/shard_map/extinction/pallas_call | solution.py:267
  2.1 0.5 %collective-permute-start = (f32[2,8,2048]{2,1,0:T(8,128)S(1)}, f32[2,8,2048]{2,1,0:T(8,128)S(1)}, u32[]{:S(2)}, u32[]{:S(2)}) collective-permute-start(f32[2,8,2048]{2,1,0:T(8,128)S(1)} %get-tuple-element.20.send_ref), channel_id=1, source_target_pairs={{0,4},{4,0},{8,12},{12,8},{16,20},{20,16},{24,28},{28,24},{1,5},{5... | collective-permute-start | bytes 393224 | tf_op jit(solution)/shard_map/ppermute | solution.py:284
  2.7 3.6 %collective-permute-start.1 = (f32[8,2048]{1,0:T(8,128)S(1)}, f32[8,2048]{1,0:T(8,128)S(1)}, u32[]{:S(2)}, u32[]{:S(2)}) collective-permute-start(f32[8,2048]{1,0:T(8,128)S(1)} %get-tuple-element.21), channel_id=1, source_target_pairs={{4,8},{12,16},{20,24},{28,0},{8,4},{16,12},{24,20},{0,28},{5,9},{1... | collective-permute-start | bytes 196616 | tf_op jit(solution)/shard_map/ppermute | solution.py:286
  6.2 0.0 collective-permute-done.pair_ref
  6.2 0.3 %collective-permute-start.2 = (f32[8,2048]{1,0:T(8,128)S(1)}, f32[8,2048]{1,0:T(8,128)S(1)}, u32[]{:S(2)}, u32[]{:S(2)}) collective-permute-start(f32[8,2048]{1,0:T(8,128)S(1)} %fusion), channel_id=1, source_target_pairs={{0,8},{4,12},{8,0},{12,4},{16,24},{20,28},{24,16},{28,20},{1,9},{5... | collective-permute-start | bytes 196616 | tf_op jit(solution)/shard_map/ppermute | solution.py:301
  6.6 1.5 %collective-permute-start.3 = (f32[8,2048]{1,0:T(8,128)S(1)}, f32[8,2048]{1,0:T(8,128)S(1)}, u32[]{:S(2)}, u32[]{:S(2)}) collective-permute-start(f32[8,2048]{1,0:T(8,128)S(1)} %fusion), channel_id=1, source_target_pairs={{0,16},{4,20},{8,24},{12,28},{16,0},{20,4},{24,8},{28,12},{1,17},{... | collective-permute-start | bytes 196616 | tf_op jit(solution)/shard_map/ppermute | solution.py:301
  8.1 1.7 %collective-permute-start.4 = (f32[8,2048]{1,0:T(8,128)S(1)}, f32[8,2048]{1,0:T(8,128)S(1)}, u32[]{:S(2)}, u32[]{:S(2)}) collective-permute-start(f32[8,2048]{1,0:T(8,128)S(1)} %fusion), channel_id=1, source_target_pairs={{0,24},{4,28},{8,16},{12,20},{16,8},{20,12},{24,0},{28,4},{1,25},{... | collective-permute-start | bytes 196616 | tf_op jit(solution)/shard_map/ppermute | solution.py:301
  9.8 1.1 %shade.1._ = f32[16,128,128]{2,1,0:T(8,128)S(1)} custom-call(f32[16,8,2048]{2,1,0:T(8,128)S(1)} %get-tuple-element.18.density_ref, f32[16,128,128]{2,1,0:T(8,128)S(1)} %get-tuple-element.19.ext_ref), custom_call_target="tpu_custom_call" | custom-call | flops 1200000 | bytes 3600000 | tf_op jit(solution)/shard_map/shade/pallas_call | solution.py:235
  10.9 1.9 %terms.1 = (f32[3,8,16,2048]{3,2,1,0:T(8,128)S(1)}, f32[16,2048]{1,0:T(8,128)S(1)}) custom-call(f32[4,128]{1,0:T(4,128)S(1)} %get-tuple-element.22.table_ref, s32[16,128,128]{2,1,0:T(8,128)S(1)} %get-tuple-element.23.entry_ref, f32[16,128,128]{2,1,0:T(8,128)S(1)} %get-tuple-element.19.ext_ref), custom_call_target="tpu_custom_call" | custom-call | flops 2500000 | bytes 7500000 | tf_op jit(solution)/shard_map/terms/pallas_call | solution.py:235
  12.8 0.0 collective-permute-done.1.edge_ref
  12.8 0.1 outer.1.shade_ref
  12.9 0.0 collective-permute-done.2.refs_0_
  12.9 0.0 collective-permute-done.3.refs_1_
  12.9 0.3 %collective-permute-done.4.refs_2_ = f32[8,2048]{1,0:T(8,128)S(1)} collective-permute-done((f32[8,2048]{1,0:T(8,128)S(1)}, f32[8,2048]{1,0:T(8,128)S(1)}, u32[]{:S(2)}, u32[]{:S(2)}) %collective-permute-start.4) | collective-permute-done | bytes 65568 | tf_op jit(solution)/shard_map/ppermute | solution.py:301
  13.2 0.2 picture.3
  13.4 1.6 %collective-permute-start.5 = (f32[4,16,512]{2,1,0:T(8,128)S(1)}, f32[4,16,512]{2,1,0:T(8,128)S(1)}, u32[]{:S(2)}, u32[]{:S(2)}) collective-permute-start(f32[4,16,512]{2,1,0:T(8,128)S(1)} %picture.3), channel_id=1, source_target_pairs={{0,1},{1,2},{2,3},{3,0},{4,5},{5,6},{6,7},{7,4},{8,9},{9,10},{10,1... | collective-permute-start | bytes 393224 | tf_op jit(solution)/shard_map/ppermute | solution.py:321
  15.1 0.5 %picture.2 = (f32[4,16,512]{2,1,0:T(8,128)S(1)}, f32[4,16,512]{2,1,0:T(8,128)S(1)}, f32[4,16,512]{2,1,0:T(8,128)S(1)}) custom-call(f32[16,128,128]{2,1,0:T(8,128)S(1)} %outer.1.shade_ref, f32[3,8,16,2048]{3,2,1,0:T(8,128)S(1)} %get-tuple-element.24.term_ref, f32[16,2048]{1,0:T(8,128)S(1)} %get-tuple-element.25.clear_ref, ...), custom_call_target="tpu_custom_call" | custom-call | flops 600000 | bytes 1800000 | tf_op jit(solution)/shard_map/picture/pallas_call | solution.py:235
  15.5 2.7 %collective-permute-start.6 = (f32[4,16,512]{2,1,0:T(8,128)S(1)}, f32[4,16,512]{2,1,0:T(8,128)S(1)}, u32[]{:S(2)}, u32[]{:S(2)}) collective-permute-start(f32[4,16,512]{2,1,0:T(8,128)S(1)} %get-tuple-element.27), channel_id=1, source_target_pairs={{0,2},{1,3},{2,0},{3,1},{4,6},{5,7},{6,4},{7,5},{8,10},{9,11},{10,... | collective-permute-start | bytes 393224 | tf_op jit(solution)/shard_map/ppermute | solution.py:321
  18.2 1.3 %collective-permute-start.7 = (f32[4,16,512]{2,1,0:T(8,128)S(1)}, f32[4,16,512]{2,1,0:T(8,128)S(1)}, u32[]{:S(2)}, u32[]{:S(2)}) collective-permute-start(f32[4,16,512]{2,1,0:T(8,128)S(1)} %get-tuple-element.28), channel_id=1, source_target_pairs={{0,3},{1,0},{2,1},{3,2},{4,7},{5,4},{6,5},{7,6},{8,11},{9,8},{10,9... | collective-permute-start | bytes 393224 | tf_op jit(solution)/shard_map/ppermute | solution.py:321
  19.5 2.1 %collective-permute-done.5.refs_1_ = f32[4,16,512]{2,1,0:T(8,128)S(1)} collective-permute-done((f32[4,16,512]{2,1,0:T(8,128)S(1)}, f32[4,16,512]{2,1,0:T(8,128)S(1)}, u32[]{:S(2)}, u32[]{:S(2)}) %collective-permute-start.5) | collective-permute-done | bytes 131104 | tf_op jit(solution)/shard_map/ppermute | solution.py:321
  21.6 3.7 %collective-permute-done.6.refs_2_ = f32[4,16,512]{2,1,0:T(8,128)S(1)} collective-permute-done((f32[4,16,512]{2,1,0:T(8,128)S(1)}, f32[4,16,512]{2,1,0:T(8,128)S(1)}, u32[]{:S(2)}, u32[]{:S(2)}) %collective-permute-start.6) | collective-permute-done | bytes 131104 | tf_op jit(solution)/shard_map/ppermute | solution.py:321
  25.3 0.0 collective-permute-done.7.refs_3_
  25.3 0.7 %combine.1 = f32[4,16,512]{2,1,0:T(8,128)} custom-call(f32[16,8,128]{2,1,0:T(8,128)S(1)} %get-tuple-element.17.front_ref, f32[4,16,512]{2,1,0:T(8,128)S(1)} %get-tuple-element.26.refs_0_, f32[4,16,512]{2,1,0:T(8,128)S(1)} %collective-permute-done.5.refs_1_, f32[4,16,512]{2,1,0:T(8,128)S(1)} %collective-permute-done.6.refs_2_, ...), custom_call_target="tpu_custom_call" | custom-call | flops 1000000 | bytes 3000000 | tf_op jit(solution)/shard_map/combine/pallas_call | solution.py:235
  (1 shorter events, 0.0 us)
Async XLA Ops:
  2.1 4.1 %collective-permute-start = (f32[2,8,2048]{2,1,0:T(8,128)S(1)}, f32[2,8,2048]{2,1,0:T(8,128)S(1)}, u32[]{:S(2)}, u32[]{:S(2)}) collective-permute-start(f32[2,8,2048]{2,1,0:T(8,128)S(1)} %get-tuple-element.20.send_ref), channel_id=1, source_target_pairs={{0,4},{4,0},{8,12},{12,8},{16,20},{20,16},{24,28},{28,24},{1,5},{5... | collective-permute-start | bytes 393224 | tf_op jit(solution)/shard_map/ppermute | solution.py:284
  2.7 10.1 %collective-permute-start.1 = (f32[8,2048]{1,0:T(8,128)S(1)}, f32[8,2048]{1,0:T(8,128)S(1)}, u32[]{:S(2)}, u32[]{:S(2)}) collective-permute-start(f32[8,2048]{1,0:T(8,128)S(1)} %get-tuple-element.21), channel_id=1, source_target_pairs={{4,8},{12,16},{20,24},{28,0},{8,4},{16,12},{24,20},{0,28},{5,9},{1... | collective-permute-start | bytes 196616 | tf_op jit(solution)/shard_map/ppermute | solution.py:286
  6.2 6.7 %collective-permute-start.2 = (f32[8,2048]{1,0:T(8,128)S(1)}, f32[8,2048]{1,0:T(8,128)S(1)}, u32[]{:S(2)}, u32[]{:S(2)}) collective-permute-start(f32[8,2048]{1,0:T(8,128)S(1)} %fusion), channel_id=1, source_target_pairs={{0,8},{4,12},{8,0},{12,4},{16,24},{20,28},{24,16},{28,20},{1,9},{5... | collective-permute-start | bytes 196616 | tf_op jit(solution)/shard_map/ppermute | solution.py:301
  6.6 6.4 %collective-permute-start.3 = (f32[8,2048]{1,0:T(8,128)S(1)}, f32[8,2048]{1,0:T(8,128)S(1)}, u32[]{:S(2)}, u32[]{:S(2)}) collective-permute-start(f32[8,2048]{1,0:T(8,128)S(1)} %fusion), channel_id=1, source_target_pairs={{0,16},{4,20},{8,24},{12,28},{16,0},{20,4},{24,8},{28,12},{1,17},{... | collective-permute-start | bytes 196616 | tf_op jit(solution)/shard_map/ppermute | solution.py:301
  8.1 5.2 %collective-permute-start.4 = (f32[8,2048]{1,0:T(8,128)S(1)}, f32[8,2048]{1,0:T(8,128)S(1)}, u32[]{:S(2)}, u32[]{:S(2)}) collective-permute-start(f32[8,2048]{1,0:T(8,128)S(1)} %fusion), channel_id=1, source_target_pairs={{0,24},{4,28},{8,16},{12,20},{16,8},{20,12},{24,0},{28,4},{1,25},{... | collective-permute-start | bytes 196616 | tf_op jit(solution)/shard_map/ppermute | solution.py:301
  13.4 8.2 %collective-permute-start.5 = (f32[4,16,512]{2,1,0:T(8,128)S(1)}, f32[4,16,512]{2,1,0:T(8,128)S(1)}, u32[]{:S(2)}, u32[]{:S(2)}) collective-permute-start(f32[4,16,512]{2,1,0:T(8,128)S(1)} %picture.3), channel_id=1, source_target_pairs={{0,1},{1,2},{2,3},{3,0},{4,5},{5,6},{6,7},{7,4},{8,9},{9,10},{10,1... | collective-permute-start | bytes 393224 | tf_op jit(solution)/shard_map/ppermute | solution.py:321
  15.5 9.8 %collective-permute-start.6 = (f32[4,16,512]{2,1,0:T(8,128)S(1)}, f32[4,16,512]{2,1,0:T(8,128)S(1)}, u32[]{:S(2)}, u32[]{:S(2)}) collective-permute-start(f32[4,16,512]{2,1,0:T(8,128)S(1)} %get-tuple-element.27), channel_id=1, source_target_pairs={{0,2},{1,3},{2,0},{3,1},{4,6},{5,7},{6,4},{7,5},{8,10},{9,11},{10,... | collective-permute-start | bytes 393224 | tf_op jit(solution)/shard_map/ppermute | solution.py:321
  18.2 7.2 %collective-permute-start.7 = (f32[4,16,512]{2,1,0:T(8,128)S(1)}, f32[4,16,512]{2,1,0:T(8,128)S(1)}, u32[]{:S(2)}, u32[]{:S(2)}) collective-permute-start(f32[4,16,512]{2,1,0:T(8,128)S(1)} %get-tuple-element.28), channel_id=1, source_target_pairs={{0,3},{1,0},{2,1},{3,2},{4,7},{5,4},{6,5},{7,6},{8,11},{9,8},{10,9... | collective-permute-start | bytes 393224 | tf_op jit(solution)/shard_map/ppermute | solution.py:321

commit v6 on v5

--- a/solution.py
+++ b/solution.py
@@ -39,8 +39,8 @@
 
 def extinction_kernel(
     tiles_along, density_hbm, bin_hbm, table_hbm, order_hbm,
-    density_ref, table_ref, entry_ref, ext_ref, send_ref, edge_ref, front_ref,
-    bin_ref, order_ref, density_sem, bin_sem, table_sem, order_sem,
+    density_ref, bin_ref, table_ref, ext_ref, send_ref, edge_ref, front_ref,
+    order_ref, density_sem, bin_sem, table_sem, order_sem,
 ):
     light_cells, _, columns = density_hbm.shape
     tiles = columns // LANES
@@ -74,7 +74,6 @@
         for tile in range(tiles):
             entry = bin_ref[i, :, lanes(tile)]
             ext = look_up(rows, entry) * density_ref[i, :, lanes(tile)]
-            entry_ref[tile, eight(i)] = entry
             ext_ref[tile, eight(i)] = ext
             sums.append(running[tile] + ext)
         return tuple(sums)
@@ -94,7 +93,7 @@
     _, depth_cells, light_cells, columns = term_ref.shape
     tables = [table_rows(table_ref, c) for c in range(3)]
 
-    @pl.loop(0, columns // LANES, unroll=4)
+    @pl.loop(0, columns // LANES, unroll=8)
     def _(tile):
         at = pl.ds(pl.multiple_of(tile * LANES, LANES), LANES)
         for half in range(0, light_cells, 8):
@@ -125,7 +124,7 @@
     return result
 
 
-def shade_kernel(light_step, density_ref, ext_ref, shade_ref):
+def shade_kernel(light_step, density_ref, bin_ref, ext_ref, shade_ref, entry_ref):
     light_cells, _, columns = density_ref.shape
     count = columns // LANES
 
@@ -139,13 +138,16 @@
         )
         for tile in range(count):
             shade_ref[tile, eight(i)] = values[tile]
+            entry_ref[tile, eight(i)] = bin_ref[i, :, lanes(tile)]
         return tuple(before[tile] + ext_ref[tile, eight(i)] for tile in range(count))
 
     for tile in range(count):
         shade_ref[tile, eight(0)] = jnp.zeros((8, LANES), F32)
         shade_ref[tile, eight(light_cells - 1)] = jnp.zeros((8, LANES), F32)
+        for i in (0, light_cells - 1):
+            entry_ref[tile, eight(i)] = bin_ref[i, :, lanes(tile)]
     before = tuple(ext_ref[tile, eight(0)] for tile in range(count))
-    lax.fori_loop(1, light_cells - 1, layer, before, unroll=2)
+    lax.fori_loop(1, light_cells - 1, layer, before, unroll=7)
 
 
 def outer_kernel(light_step, light_count, density_ref, ext_ref, send_ref, pair_ref, edge_ref, _, shade_ref):
@@ -185,8 +187,9 @@
     mine = lax.axis_index("tile")
     place = lax.axis_index("light")
     upstream = jnp.where((place & 1) > 0, pair_ref[0], 0.0)
-    for mask, group_ref in zip(masks, group_refs):
-        upstream = upstream + jnp.where((place ^ mask) < place, group_ref[...], 0.0)
+    for (even, odd), group_ref in zip(masks, group_refs):
+        source = place ^ jnp.where((place & 1) > 0, odd, even)
+        upstream = upstream + jnp.where(source < place, group_ref[...], 0.0)
     fade_ref[...] = jnp.exp2(upstream * (-light_step * LOG2E))
     for step, out_ref in zip(steps, out_refs):
         owner = lax.rem(mine + step, tiles)
@@ -261,16 +264,15 @@
     hbm = pl.BlockSpec(memory_space=pltpu.HBM)
     vmem = pl.BlockSpec(memory_space=pltpu.VMEM)
     outs = [
-        shape(*density.shape), shape(*transfer.shape), shape(*tiled, dtype=jnp.int32), shape(*tiled),
+        shape(*density.shape), shape(*density.shape, dtype=jnp.int32), shape(*transfer.shape), shape(*tiled),
         shape(2, *plane.shape), plane, shape(tile_count * tile_count, 8, LANES),
     ]
-    dense, table, entry, ext, send, edge, front = pl.pallas_call(
+    dense, bins, table, ext, send, edge, front = pl.pallas_call(
         functools.partial(extinction_kernel, tile_count),
         out_shape=outs,
         in_specs=[hbm] * 4,
         out_specs=[vmem] * len(outs),
         scratch_shapes=[
-            pltpu.VMEM(bin_index.shape, jnp.int32),
             pltpu.SMEM(depth_order.shape, jnp.int32),
             pltpu.SemaphoreType.DMA((2,)),
             pltpu.SemaphoreType.DMA((2,)),
@@ -284,21 +286,24 @@
     pair = lax.ppermute(send, "light", [(i, i ^ 1) for i in range(light_count)])
     beside = [(i, (i + 1) % light_count) for i in range(1, light_count, 2)]
     edge = lax.ppermute(edge, "light", beside + [(b, a) for a, b in beside])
+    shade, entry = call(
+        functools.partial(shade_kernel, light_step), [shape(*tiled), shape(*tiled, dtype=jnp.int32)],
+        (dense, bins, ext), "shade", cost=1.2,
+    )
     term, clear = call(
         functools.partial(terms_kernel, view_step),
         [shape(3, depth_cells, light_cells, columns), shape(light_cells, columns)],
         (table, entry, ext), "terms", cost=2.5,
-    )
-    shade = call(
-        functools.partial(shade_kernel, light_step), shape(*tiled), (dense, ext), "shade", cost=1.2
     )
     group = send[0] + pair[0]
     groups = []
     masks = []
     step = 2
     while step < light_count:
-        reach = [m * step for m in (1, 2, 3)] if step * 4 <= light_count else [step]
-        got = [lax.ppermute(group, "light", [(i, i ^ m) for i in range(light_count)]) for m in reach]
+        reach = [(a * step, b * step) for a, b in ((1, 2), (2, 1), (3, 3))] if step * 4 <= light_count else [(step, step)]
+        got = [
+            lax.ppermute(group, "light", [(i, i ^ masks_of[i % 2]) for i in range(light_count)]) for masks_of in reach
+        ]
         groups += got
         masks += reach
         group = group + functools.reduce(jnp.add, got)

time: 26.2 us -> 26.2 us (level)
  Pallas kernels: 6.59 us -> 6.12 us
  waiting for transfers between devices: 6.13 us -> 6.56 us
    pallas_call x6, Pallas kernels: 4.47 us -> 4.01 us  [call(): pl.pallas_call(kernel, out_shape=outs, in_specs=[pl.BlockSpec(memory_spac...]
    ppermute x3, waiting for transfers between devices: 0.31 us -> 0.74 us  [per_device(): lax.ppermute(group, 'light', [(i, i ^ masks_of[i % 2]) for i in range(lig...]
  transfers between devices with their start and end apart: 8 -> 8, of which waited for: 3 -> 3; matrix products, arithmetic and copies ran while one was open for 0% -> 0% of each run, Pallas kernels for 14% -> 12%
where the time goes in v6:
time: 26.2 us; the launch traced here: 26 us
  starting transfers between devices  13.3 us (51%)
  waiting for transfers between devices  6.56 us (25%)
  Pallas kernels  6.12 us (23%)
    ppermute x3, waiting for transfers between devices, per_device(): lax.ppermute(piece, 'tile', [(i, (i + step) % tile_count) for i in range(...  5.81 us
    ppermute x3, starting transfers between devices, per_device(): lax.ppermute(piece, 'tile', [(i, (i + step) % tile_count) for i in range(...  5.63 us
    pallas_call x6, Pallas kernels, call(): pl.pallas_call(kernel, out_shape=outs, in_specs=[pl.BlockSpec(memory_spac...  4.01 us
    ppermute x3, starting transfers between devices, per_device(): lax.ppermute(group, 'light', [(i, i ^ masks_of[i % 2]) for i in range(lig...  3.57 us
    ppermute x1, starting transfers between devices, per_device(): edge = lax.ppermute(edge, 'light', beside + [(b, a) for a, b in beside])  3.56 us
    pallas_call x1, Pallas kernels, per_device(): pl.pallas_call(functools.partial(extinction_kernel, tile_count), out_shap...  2.11 us
    ppermute x3, waiting for transfers between devices, per_device(): lax.ppermute(group, 'light', [(i, i ^ masks_of[i % 2]) for i in range(lig...  0.74 us
  transfers between devices with their start and end apart: 8, of which 3 were waited for; matrix products, arithmetic and copies ran while one was open for 0% of the time, Pallas kernels for 12%

profile of v6, /device:TPU:0, one launch (start us, length us, event | category | flops | bytes accessed | tf_op | source)
XLA Modules:
  0.0 26.0 jit_solution(1355945903423892049)
XLA Ops:
  0.0 2.1 %extinction.1 = (f32[16,8,2048]{2,1,0:T(8,128)S(1)}, s32[16,8,2048]{2,1,0:T(8,128)S(1)}, f32[4,128]{1,0:T(4,128)S(1)}, f32[16,128,128]{2,1,0:T(8,128)S(1)}, f32[...) custom-call(f32[16,8,2048]{2,1,0:T(8,128)} %density_hbm.1, s32[16,8,2048]{2,1,0:T(8,128)} %bin_hbm.1, ...), custom_call_target="tpu_custom_call" | custom-call | tf_op jit(solution)/shard_map/extinction/pallas_call | solution.py:270
  2.1 0.5 %collective-permute-start = (f32[2,8,2048]{2,1,0:T(8,128)S(1)}, f32[2,8,2048]{2,1,0:T(8,128)S(1)}, u32[]{:S(2)}, u32[]{:S(2)}) collective-permute-start(f32[2,8,2048]{2,1,0:T(8,128)S(1)} %get-tuple-element.22.send_ref), channel_id=1, source_target_pairs={{0,4},{4,0},{8,12},{12,8},{16,20},{20,16},{24,28},{28,24},{1,5},{5... | collective-permute-start | bytes 393224 | tf_op jit(solution)/shard_map/ppermute | solution.py:286
  2.6 3.6 %collective-permute-start.1 = (f32[8,2048]{1,0:T(8,128)S(1)}, f32[8,2048]{1,0:T(8,128)S(1)}, u32[]{:S(2)}, u32[]{:S(2)}) collective-permute-start(f32[8,2048]{1,0:T(8,128)S(1)} %get-tuple-element.23), channel_id=1, source_target_pairs={{4,8},{12,16},{20,24},{28,0},{8,4},{16,12},{24,20},{0,28},{5,9},{1... | collective-permute-start | bytes 196616 | tf_op jit(solution)/shard_map/ppermute | solution.py:288
  6.2 0.0 collective-permute-done.pair_ref
  6.2 0.3 %collective-permute-start.2 = (f32[8,2048]{1,0:T(8,128)S(1)}, f32[8,2048]{1,0:T(8,128)S(1)}, u32[]{:S(2)}, u32[]{:S(2)}) collective-permute-start(f32[8,2048]{1,0:T(8,128)S(1)} %fusion), channel_id=1, source_target_pairs={{0,8},{4,20},{8,0},{12,28},{16,24},{20,4},{24,16},{28,12},{1,9},{5... | collective-permute-start | bytes 196616 | tf_op jit(solution)/shard_map/ppermute | solution.py:305
  6.6 1.5 %collective-permute-start.3 = (f32[8,2048]{1,0:T(8,128)S(1)}, f32[8,2048]{1,0:T(8,128)S(1)}, u32[]{:S(2)}, u32[]{:S(2)}) collective-permute-start(f32[8,2048]{1,0:T(8,128)S(1)} %fusion), channel_id=1, source_target_pairs={{0,16},{4,12},{8,24},{12,4},{16,0},{20,28},{24,8},{28,20},{1,17},{... | collective-permute-start | bytes 196616 | tf_op jit(solution)/shard_map/ppermute | solution.py:305
  8.1 1.7 %collective-permute-start.4 = (f32[8,2048]{1,0:T(8,128)S(1)}, f32[8,2048]{1,0:T(8,128)S(1)}, u32[]{:S(2)}, u32[]{:S(2)}) collective-permute-start(f32[8,2048]{1,0:T(8,128)S(1)} %fusion), channel_id=1, source_target_pairs={{0,24},{4,28},{8,16},{12,20},{16,8},{20,12},{24,0},{28,4},{1,25},{... | collective-permute-start | bytes 196616 | tf_op jit(solution)/shard_map/ppermute | solution.py:305
  9.8 0.8 %shade.1 = (f32[16,128,128]{2,1,0:T(8,128)S(1)}, s32[16,128,128]{2,1,0:T(8,128)S(1)}) custom-call(f32[16,8,2048]{2,1,0:T(8,128)S(1)} %get-tuple-element.20.density_ref, s32[16,8,2048]{2,1,0:T(8,128)S(1)} %get-tuple-element.24.bin_ref, f32[16,128,128]{2,1,0:T(8,128)S(1)} %get-tuple-element.21.ext_ref), custom_call_target="tpu_custom_call" | custom-call | flops 1200000 | bytes 3600000 | tf_op jit(solution)/shard_map/shade/pallas_call | solution.py:238
  10.6 1.8 %terms.1 = (f32[3,8,16,2048]{3,2,1,0:T(8,128)S(1)}, f32[16,2048]{1,0:T(8,128)S(1)}) custom-call(f32[4,128]{1,0:T(4,128)S(1)} %get-tuple-element.26.table_ref, s32[16,128,128]{2,1,0:T(8,128)S(1)} %get-tuple-element.27.entry_ref, f32[16,128,128]{2,1,0:T(8,128)S(1)} %get-tuple-element.21.ext_ref), custom_call_target="tpu_custom_call" | custom-call | flops 2500000 | bytes 7500000 | tf_op jit(solution)/shard_map/terms/pallas_call | solution.py:238
  12.3 0.0 collective-permute-done.1.edge_ref
  12.3 0.1 outer.1.shade_ref
  12.5 0.0 collective-permute-done.2.refs_0_
  12.5 0.0 collective-permute-done.3.refs_1_
  12.5 0.7 %collective-permute-done.4.refs_2_ = f32[8,2048]{1,0:T(8,128)S(1)} collective-permute-done((f32[8,2048]{1,0:T(8,128)S(1)}, f32[8,2048]{1,0:T(8,128)S(1)}, u32[]{:S(2)}, u32[]{:S(2)}) %collective-permute-start.4) | collective-permute-done | bytes 65568 | tf_op jit(solution)/shard_map/ppermute | solution.py:305
  13.2 0.2 picture.3
  13.4 1.6 %collective-permute-start.5 = (f32[4,16,512]{2,1,0:T(8,128)S(1)}, f32[4,16,512]{2,1,0:T(8,128)S(1)}, u32[]{:S(2)}, u32[]{:S(2)}) collective-permute-start(f32[4,16,512]{2,1,0:T(8,128)S(1)} %picture.3), channel_id=1, source_target_pairs={{0,1},{1,2},{2,3},{3,0},{4,5},{5,6},{6,7},{7,4},{8,9},{9,10},{10,1... | collective-permute-start | bytes 393224 | tf_op jit(solution)/shard_map/ppermute | solution.py:326
  15.0 0.5 %picture.2 = (f32[4,16,512]{2,1,0:T(8,128)S(1)}, f32[4,16,512]{2,1,0:T(8,128)S(1)}, f32[4,16,512]{2,1,0:T(8,128)S(1)}) custom-call(f32[16,128,128]{2,1,0:T(8,128)S(1)} %outer.1.shade_ref, f32[3,8,16,2048]{3,2,1,0:T(8,128)S(1)} %get-tuple-element.28.term_ref, f32[16,2048]{1,0:T(8,128)S(1)} %get-tuple-element.29.clear_ref, ...), custom_call_target="tpu_custom_call" | custom-call | flops 600000 | bytes 1800000 | tf_op jit(solution)/shard_map/picture/pallas_call | solution.py:238
  15.5 2.7 %collective-permute-start.6 = (f32[4,16,512]{2,1,0:T(8,128)S(1)}, f32[4,16,512]{2,1,0:T(8,128)S(1)}, u32[]{:S(2)}, u32[]{:S(2)}) collective-permute-start(f32[4,16,512]{2,1,0:T(8,128)S(1)} %get-tuple-element.31), channel_id=1, source_target_pairs={{0,2},{1,3},{2,0},{3,1},{4,6},{5,7},{6,4},{7,5},{8,10},{9,11},{10,... | collective-permute-start | bytes 393224 | tf_op jit(solution)/shard_map/ppermute | solution.py:326
  18.2 1.3 %collective-permute-start.7 = (f32[4,16,512]{2,1,0:T(8,128)S(1)}, f32[4,16,512]{2,1,0:T(8,128)S(1)}, u32[]{:S(2)}, u32[]{:S(2)}) collective-permute-start(f32[4,16,512]{2,1,0:T(8,128)S(1)} %get-tuple-element.32), channel_id=1, source_target_pairs={{0,3},{1,0},{2,1},{3,2},{4,7},{5,4},{6,5},{7,6},{8,11},{9,8},{10,9... | collective-permute-start | bytes 393224 | tf_op jit(solution)/shard_map/ppermute | solution.py:326
  19.5 2.1 %collective-permute-done.5.refs_1_ = f32[4,16,512]{2,1,0:T(8,128)S(1)} collective-permute-done((f32[4,16,512]{2,1,0:T(8,128)S(1)}, f32[4,16,512]{2,1,0:T(8,128)S(1)}, u32[]{:S(2)}, u32[]{:S(2)}) %collective-permute-start.5) | collective-permute-done | bytes 131104 | tf_op jit(solution)/shard_map/ppermute | solution.py:326
  21.6 3.7 %collective-permute-done.6.refs_2_ = f32[4,16,512]{2,1,0:T(8,128)S(1)} collective-permute-done((f32[4,16,512]{2,1,0:T(8,128)S(1)}, f32[4,16,512]{2,1,0:T(8,128)S(1)}, u32[]{:S(2)}, u32[]{:S(2)}) %collective-permute-start.6) | collective-permute-done | bytes 131104 | tf_op jit(solution)/shard_map/ppermute | solution.py:326
  25.3 0.0 collective-permute-done.7.refs_3_
  25.3 0.7 %combine.1 = f32[4,16,512]{2,1,0:T(8,128)} custom-call(f32[16,8,128]{2,1,0:T(8,128)S(1)} %get-tuple-element.19.front_ref, f32[4,16,512]{2,1,0:T(8,128)S(1)} %get-tuple-element.30.refs_0_, f32[4,16,512]{2,1,0:T(8,128)S(1)} %collective-permute-done.5.refs_1_, f32[4,16,512]{2,1,0:T(8,128)S(1)} %collective-permute-done.6.refs_2_, ...), custom_call_target="tpu_custom_call" | custom-call | flops 1000000 | bytes 3000000 | tf_op jit(solution)/shard_map/combine/pallas_call | solution.py:238
  (1 shorter events, 0.0 us)
Async XLA Ops:
  2.1 4.1 %collective-permute-start = (f32[2,8,2048]{2,1,0:T(8,128)S(1)}, f32[2,8,2048]{2,1,0:T(8,128)S(1)}, u32[]{:S(2)}, u32[]{:S(2)}) collective-permute-start(f32[2,8,2048]{2,1,0:T(8,128)S(1)} %get-tuple-element.22.send_ref), channel_id=1, source_target_pairs={{0,4},{4,0},{8,12},{12,8},{16,20},{20,16},{24,28},{28,24},{1,5},{5... | collective-permute-start | bytes 393224 | tf_op jit(solution)/shard_map/ppermute | solution.py:286
  2.6 9.7 %collective-permute-start.1 = (f32[8,2048]{1,0:T(8,128)S(1)}, f32[8,2048]{1,0:T(8,128)S(1)}, u32[]{:S(2)}, u32[]{:S(2)}) collective-permute-start(f32[8,2048]{1,0:T(8,128)S(1)} %get-tuple-element.23), channel_id=1, source_target_pairs={{4,8},{12,16},{20,24},{28,0},{8,4},{16,12},{24,20},{0,28},{5,9},{1... | collective-permute-start | bytes 196616 | tf_op jit(solution)/shard_map/ppermute | solution.py:288
  6.2 6.3 %collective-permute-start.2 = (f32[8,2048]{1,0:T(8,128)S(1)}, f32[8,2048]{1,0:T(8,128)S(1)}, u32[]{:S(2)}, u32[]{:S(2)}) collective-permute-start(f32[8,2048]{1,0:T(8,128)S(1)} %fusion), channel_id=1, source_target_pairs={{0,8},{4,20},{8,0},{12,28},{16,24},{20,4},{24,16},{28,12},{1,9},{5... | collective-permute-start | bytes 196616 | tf_op jit(solution)/shard_map/ppermute | solution.py:305
  6.6 5.9 %collective-permute-start.3 = (f32[8,2048]{1,0:T(8,128)S(1)}, f32[8,2048]{1,0:T(8,128)S(1)}, u32[]{:S(2)}, u32[]{:S(2)}) collective-permute-start(f32[8,2048]{1,0:T(8,128)S(1)} %fusion), channel_id=1, source_target_pairs={{0,16},{4,12},{8,24},{12,4},{16,0},{20,28},{24,8},{28,20},{1,17},{... | collective-permute-start | bytes 196616 | tf_op jit(solution)/shard_map/ppermute | solution.py:305
  8.1 5.2 %collective-permute-start.4 = (f32[8,2048]{1,0:T(8,128)S(1)}, f32[8,2048]{1,0:T(8,128)S(1)}, u32[]{:S(2)}, u32[]{:S(2)}) collective-permute-start(f32[8,2048]{1,0:T(8,128)S(1)} %fusion), channel_id=1, source_target_pairs={{0,24},{4,28},{8,16},{12,20},{16,8},{20,12},{24,0},{28,4},{1,25},{... | collective-permute-start | bytes 196616 | tf_op jit(solution)/shard_map/ppermute | solution.py:305
  13.4 8.2 %collective-permute-start.5 = (f32[4,16,512]{2,1,0:T(8,128)S(1)}, f32[4,16,512]{2,1,0:T(8,128)S(1)}, u32[]{:S(2)}, u32[]{:S(2)}) collective-permute-start(f32[4,16,512]{2,1,0:T(8,128)S(1)} %picture.3), channel_id=1, source_target_pairs={{0,1},{1,2},{2,3},{3,0},{4,5},{5,6},{6,7},{7,4},{8,9},{9,10},{10,1... | collective-permute-start | bytes 393224 | tf_op jit(solution)/shard_map/ppermute | solution.py:326
  15.5 9.8 %collective-permute-start.6 = (f32[4,16,512]{2,1,0:T(8,128)S(1)}, f32[4,16,512]{2,1,0:T(8,128)S(1)}, u32[]{:S(2)}, u32[]{:S(2)}) collective-permute-start(f32[4,16,512]{2,1,0:T(8,128)S(1)} %get-tuple-element.31), channel_id=1, source_target_pairs={{0,2},{1,3},{2,0},{3,1},{4,6},{5,7},{6,4},{7,5},{8,10},{9,11},{10,... | collective-permute-start | bytes 393224 | tf_op jit(solution)/shard_map/ppermute | solution.py:326
  18.2 7.2 %collective-permute-start.7 = (f32[4,16,512]{2,1,0:T(8,128)S(1)}, f32[4,16,512]{2,1,0:T(8,128)S(1)}, u32[]{:S(2)}, u32[]{:S(2)}) collective-permute-start(f32[4,16,512]{2,1,0:T(8,128)S(1)} %get-tuple-element.32), channel_id=1, source_target_pairs={{0,3},{1,0},{2,1},{3,2},{4,7},{5,4},{6,5},{7,6},{8,11},{9,8},{10,9... | collective-permute-start | bytes 393224 | tf_op jit(solution)/shard_map/ppermute | solution.py:326

commit v7 on v5

--- a/solution.py
+++ b/solution.py
@@ -308,7 +308,7 @@
         (dense, ext, send, pair, edge, shade), "outer", cost=0.2, aliases={5: 0},
     )
     held = {}
-    for steps in ([1], [*range(2, tile_count), 0]):
+    for steps in ([1], [*range(2, tile_count)], [0]):
         pieces = call(
             functools.partial(picture_kernel, light_step, tile_count, masks, steps),
             [shape(4, light_cells, share)] * len(steps),

time: 26.2 us -> 26 us (level)
    pallas_call x6 -> x7, Pallas kernels: 4.47 us -> 4.48 us  [call(): pl.pallas_call(kernel, out_shape=outs, in_specs=[pl.BlockSpec(memory_spac...]
  transfers between devices with their start and end apart: 8 -> 8, of which waited for: 3 -> 4; matrix products, arithmetic and copies ran while one was open for 0% -> 0% of each run, Pallas kernels for 14% -> 14%
where the time goes in v7:
time: 26 us; the launch traced here: 25.9 us
  starting transfers between devices  13.3 us (51%)
  Pallas kernels  6.61 us (25%)
  waiting for transfers between devices  5.95 us (23%)
    ppermute x3, waiting for transfers between devices, per_device(): lax.ppermute(piece, 'tile', [(i, (i + step) % tile_count) for i in range(...  5.63 us
    ppermute x3, starting transfers between devices, per_device(): lax.ppermute(piece, 'tile', [(i, (i + step) % tile_count) for i in range(...  5.63 us
    pallas_call x7, Pallas kernels, call(): pl.pallas_call(kernel, out_shape=outs, in_specs=[pl.BlockSpec(memory_spac...  4.48 us
    ppermute x1, starting transfers between devices, per_device(): edge = lax.ppermute(edge, 'light', beside + [(b, a) for a, b in beside])  3.56 us
    ppermute x3, starting transfers between devices, per_device(): lax.ppermute(group, 'light', [(i, i ^ m) for i in range(light_count)])  3.55 us
    pallas_call x1, Pallas kernels, per_device(): pl.pallas_call(functools.partial(extinction_kernel, tile_count), out_shap...  2.13 us
  transfers between devices with their start and end apart: 8, of which 4 were waited for; matrix products, arithmetic and copies ran while one was open for 0% of the time, Pallas kernels for 14%

profile of v7, /device:TPU:0, one launch (start us, length us, event | category | flops | bytes accessed | tf_op | source)
XLA Modules:
  0.0 25.9 jit_solution(9304710329879239931)
XLA Ops:
  0.0 2.1 %extinction.1 = (f32[16,8,2048]{2,1,0:T(8,128)S(1)}, f32[4,128]{1,0:T(4,128)S(1)}, s32[16,128,128]{2,1,0:T(8,128)S(1)}, f32[16,128,128]{2,1,0:T(8,128)S(1)}, f32...) custom-call(f32[16,8,2048]{2,1,0:T(8,128)} %density_hbm.1, s32[16,8,2048]{2,1,0:T(8,128)} %bin_hbm.1, ...), custom_call_target="tpu_custom_call" | custom-call | tf_op jit(solution)/shard_map/extinction/pallas_call | solution.py:267
  2.1 0.5 %collective-permute-start = (f32[2,8,2048]{2,1,0:T(8,128)S(1)}, f32[2,8,2048]{2,1,0:T(8,128)S(1)}, u32[]{:S(2)}, u32[]{:S(2)}) collective-permute-start(f32[2,8,2048]{2,1,0:T(8,128)S(1)} %get-tuple-element.19.send_ref), channel_id=1, source_target_pairs={{0,4},{4,0},{8,12},{12,8},{16,20},{20,16},{24,28},{28,24},{1,5},{5... | collective-permute-start | bytes 393224 | tf_op jit(solution)/shard_map/ppermute | solution.py:284
  2.7 3.6 %collective-permute-start.1 = (f32[8,2048]{1,0:T(8,128)S(1)}, f32[8,2048]{1,0:T(8,128)S(1)}, u32[]{:S(2)}, u32[]{:S(2)}) collective-permute-start(f32[8,2048]{1,0:T(8,128)S(1)} %get-tuple-element.20), channel_id=1, source_target_pairs={{4,8},{12,16},{20,24},{28,0},{8,4},{16,12},{24,20},{0,28},{5,9},{1... | collective-permute-start | bytes 196616 | tf_op jit(solution)/shard_map/ppermute | solution.py:286
  6.2 0.0 collective-permute-done.pair_ref
  6.2 0.3 %collective-permute-start.2 = (f32[8,2048]{1,0:T(8,128)S(1)}, f32[8,2048]{1,0:T(8,128)S(1)}, u32[]{:S(2)}, u32[]{:S(2)}) collective-permute-start(f32[8,2048]{1,0:T(8,128)S(1)} %fusion), channel_id=1, source_target_pairs={{0,8},{4,12},{8,0},{12,4},{16,24},{20,28},{24,16},{28,20},{1,9},{5... | collective-permute-start | bytes 196616 | tf_op jit(solution)/shard_map/ppermute | solution.py:301
  6.6 1.5 %collective-permute-start.3 = (f32[8,2048]{1,0:T(8,128)S(1)}, f32[8,2048]{1,0:T(8,128)S(1)}, u32[]{:S(2)}, u32[]{:S(2)}) collective-permute-start(f32[8,2048]{1,0:T(8,128)S(1)} %fusion), channel_id=1, source_target_pairs={{0,16},{4,20},{8,24},{12,28},{16,0},{20,4},{24,8},{28,12},{1,17},{... | collective-permute-start | bytes 196616 | tf_op jit(solution)/shard_map/ppermute | solution.py:301
  8.1 1.7 %collective-permute-start.4 = (f32[8,2048]{1,0:T(8,128)S(1)}, f32[8,2048]{1,0:T(8,128)S(1)}, u32[]{:S(2)}, u32[]{:S(2)}) collective-permute-start(f32[8,2048]{1,0:T(8,128)S(1)} %fusion), channel_id=1, source_target_pairs={{0,24},{4,28},{8,16},{12,20},{16,8},{20,12},{24,0},{28,4},{1,25},{... | collective-permute-start | bytes 196616 | tf_op jit(solution)/shard_map/ppermute | solution.py:301
  9.8 1.1 %shade.1._ = f32[16,128,128]{2,1,0:T(8,128)S(1)} custom-call(f32[16,8,2048]{2,1,0:T(8,128)S(1)} %get-tuple-element.17.density_ref, f32[16,128,128]{2,1,0:T(8,128)S(1)} %get-tuple-element.18.ext_ref), custom_call_target="tpu_custom_call" | custom-call | flops 1200000 | bytes 3600000 | tf_op jit(solution)/shard_map/shade/pallas_call | solution.py:235
  10.9 1.9 %terms.1 = (f32[3,8,16,2048]{3,2,1,0:T(8,128)S(1)}, f32[16,2048]{1,0:T(8,128)S(1)}) custom-call(f32[4,128]{1,0:T(4,128)S(1)} %get-tuple-element.21.table_ref, s32[16,128,128]{2,1,0:T(8,128)S(1)} %get-tuple-element.22.entry_ref, f32[16,128,128]{2,1,0:T(8,128)S(1)} %get-tuple-element.18.ext_ref), custom_call_target="tpu_custom_call" | custom-call | flops 2500000 | bytes 7500000 | tf_op jit(solution)/shard_map/terms/pallas_call | solution.py:235
  12.8 0.0 collective-permute-done.1.edge_ref
  12.8 0.1 outer.1.shade_ref
  12.9 0.0 collective-permute-done.2.refs_0_
  12.9 0.0 collective-permute-done.3.refs_1_
  12.9 0.3 %collective-permute-done.4.refs_2_ = f32[8,2048]{1,0:T(8,128)S(1)} collective-permute-done((f32[8,2048]{1,0:T(8,128)S(1)}, f32[8,2048]{1,0:T(8,128)S(1)}, u32[]{:S(2)}, u32[]{:S(2)}) %collective-permute-start.4) | collective-permute-done | bytes 65568 | tf_op jit(solution)/shard_map/ppermute | solution.py:301
  13.2 0.2 picture.4
  13.4 1.6 %collective-permute-start.5 = (f32[4,16,512]{2,1,0:T(8,128)S(1)}, f32[4,16,512]{2,1,0:T(8,128)S(1)}, u32[]{:S(2)}, u32[]{:S(2)}) collective-permute-start(f32[4,16,512]{2,1,0:T(8,128)S(1)} %picture.4), channel_id=1, source_target_pairs={{0,1},{1,2},{2,3},{3,0},{4,5},{5,6},{6,7},{7,4},{8,9},{9,10},{10,1... | collective-permute-start | bytes 393224 | tf_op jit(solution)/shard_map/ppermute | solution.py:321
  15.1 0.3 %picture.5 = (f32[4,16,512]{2,1,0:T(8,128)S(1)}, f32[4,16,512]{2,1,0:T(8,128)S(1)}) custom-call(f32[16,128,128]{2,1,0:T(8,128)S(1)} %outer.1.shade_ref, f32[3,8,16,2048]{3,2,1,0:T(8,128)S(1)} %get-tuple-element.23.term_ref, f32[16,2048]{1,0:T(8,128)S(1)} %get-tuple-element.24.clear_ref, f32[2,8,2048]{2,1,0:T(8,128)S(1)} %collective-permute-done.pair_ref, ...), custom_call_target="tpu_custom_call" | custom-call | flops 400000 | bytes 1200000 | tf_op jit(solution)/shard_map/picture/pallas_call | solution.py:235
  15.4 2.7 %collective-permute-start.6 = (f32[4,16,512]{2,1,0:T(8,128)S(1)}, f32[4,16,512]{2,1,0:T(8,128)S(1)}, u32[]{:S(2)}, u32[]{:S(2)}) collective-permute-start(f32[4,16,512]{2,1,0:T(8,128)S(1)} %get-tuple-element.25), channel_id=1, source_target_pairs={{0,2},{1,3},{2,0},{3,1},{4,6},{5,7},{6,4},{7,5},{8,10},{9,11},{10,... | collective-permute-start | bytes 393224 | tf_op jit(solution)/shard_map/ppermute | solution.py:321
  18.0 1.3 %collective-permute-start.7 = (f32[4,16,512]{2,1,0:T(8,128)S(1)}, f32[4,16,512]{2,1,0:T(8,128)S(1)}, u32[]{:S(2)}, u32[]{:S(2)}) collective-permute-start(f32[4,16,512]{2,1,0:T(8,128)S(1)} %get-tuple-element.26), channel_id=1, source_target_pairs={{0,3},{1,0},{2,1},{3,2},{4,7},{5,4},{6,5},{7,6},{8,11},{9,8},{10,9... | collective-permute-start | bytes 393224 | tf_op jit(solution)/shard_map/ppermute | solution.py:321
  19.4 0.2 picture.3.refs_0_
  19.6 2.1 %collective-permute-done.5.refs_1_ = f32[4,16,512]{2,1,0:T(8,128)S(1)} collective-permute-done((f32[4,16,512]{2,1,0:T(8,128)S(1)}, f32[4,16,512]{2,1,0:T(8,128)S(1)}, u32[]{:S(2)}, u32[]{:S(2)}) %collective-permute-start.5) | collective-permute-done | bytes 131104 | tf_op jit(solution)/shard_map/ppermute | solution.py:321
  21.7 3.5 %collective-permute-done.6.refs_2_ = f32[4,16,512]{2,1,0:T(8,128)S(1)} collective-permute-done((f32[4,16,512]{2,1,0:T(8,128)S(1)}, f32[4,16,512]{2,1,0:T(8,128)S(1)}, u32[]{:S(2)}, u32[]{:S(2)}) %collective-permute-start.6) | collective-permute-done | bytes 131104 | tf_op jit(solution)/shard_map/ppermute | solution.py:321
  25.1 0.1 collective-permute-done.7.refs_3_
  25.2 0.7 %combine.1 = f32[4,16,512]{2,1,0:T(8,128)} custom-call(f32[16,8,128]{2,1,0:T(8,128)S(1)} %get-tuple-element.16.front_ref, f32[4,16,512]{2,1,0:T(8,128)S(1)} %picture.3.refs_0_, f32[4,16,512]{2,1,0:T(8,128)S(1)} %collective-permute-done.5.refs_1_, f32[4,16,512]{2,1,0:T(8,128)S(1)} %collective-permute-done.6.refs_2_, ...), custom_call_target="tpu_custom_call" | custom-call | flops 1000000 | bytes 3000000 | tf_op jit(solution)/shard_map/combine/pallas_call | solution.py:235
  (1 shorter events, 0.0 us)
Async XLA Ops:
  2.1 4.1 %collective-permute-start = (f32[2,8,2048]{2,1,0:T(8,128)S(1)}, f32[2,8,2048]{2,1,0:T(8,128)S(1)}, u32[]{:S(2)}, u32[]{:S(2)}) collective-permute-start(f32[2,8,2048]{2,1,0:T(8,128)S(1)} %get-tuple-element.19.send_ref), channel_id=1, source_target_pairs={{0,4},{4,0},{8,12},{12,8},{16,20},{20,16},{24,28},{28,24},{1,5},{5... | collective-permute-start | bytes 393224 | tf_op jit(solution)/shard_map/ppermute | solution.py:284
  2.7 10.1 %collective-permute-start.1 = (f32[8,2048]{1,0:T(8,128)S(1)}, f32[8,2048]{1,0:T(8,128)S(1)}, u32[]{:S(2)}, u32[]{:S(2)}) collective-permute-start(f32[8,2048]{1,0:T(8,128)S(1)} %get-tuple-element.20), channel_id=1, source_target_pairs={{4,8},{12,16},{20,24},{28,0},{8,4},{16,12},{24,20},{0,28},{5,9},{1... | collective-permute-start | bytes 196616 | tf_op jit(solution)/shard_map/ppermute | solution.py:286
  6.2 6.7 %collective-permute-start.2 = (f32[8,2048]{1,0:T(8,128)S(1)}, f32[8,2048]{1,0:T(8,128)S(1)}, u32[]{:S(2)}, u32[]{:S(2)}) collective-permute-start(f32[8,2048]{1,0:T(8,128)S(1)} %fusion), channel_id=1, source_target_pairs={{0,8},{4,12},{8,0},{12,4},{16,24},{20,28},{24,16},{28,20},{1,9},{5... | collective-permute-start | bytes 196616 | tf_op jit(solution)/shard_map/ppermute | solution.py:301
  6.6 6.4 %collective-permute-start.3 = (f32[8,2048]{1,0:T(8,128)S(1)}, f32[8,2048]{1,0:T(8,128)S(1)}, u32[]{:S(2)}, u32[]{:S(2)}) collective-permute-start(f32[8,2048]{1,0:T(8,128)S(1)} %fusion), channel_id=1, source_target_pairs={{0,16},{4,20},{8,24},{12,28},{16,0},{20,4},{24,8},{28,12},{1,17},{... | collective-permute-start | bytes 196616 | tf_op jit(solution)/shard_map/ppermute | solution.py:301
  8.1 5.2 %collective-permute-start.4 = (f32[8,2048]{1,0:T(8,128)S(1)}, f32[8,2048]{1,0:T(8,128)S(1)}, u32[]{:S(2)}, u32[]{:S(2)}) collective-permute-start(f32[8,2048]{1,0:T(8,128)S(1)} %fusion), channel_id=1, source_target_pairs={{0,24},{4,28},{8,16},{12,20},{16,8},{20,12},{24,0},{28,4},{1,25},{... | collective-permute-start | bytes 196616 | tf_op jit(solution)/shard_map/ppermute | solution.py:301
  13.4 8.2 %collective-permute-start.5 = (f32[4,16,512]{2,1,0:T(8,128)S(1)}, f32[4,16,512]{2,1,0:T(8,128)S(1)}, u32[]{:S(2)}, u32[]{:S(2)}) collective-permute-start(f32[4,16,512]{2,1,0:T(8,128)S(1)} %picture.4), channel_id=1, source_target_pairs={{0,1},{1,2},{2,3},{3,0},{4,5},{5,6},{6,7},{7,4},{8,9},{9,10},{10,1... | collective-permute-start | bytes 393224 | tf_op jit(solution)/shard_map/ppermute | solution.py:321
  15.4 9.8 %collective-permute-start.6 = (f32[4,16,512]{2,1,0:T(8,128)S(1)}, f32[4,16,512]{2,1,0:T(8,128)S(1)}, u32[]{:S(2)}, u32[]{:S(2)}) collective-permute-start(f32[4,16,512]{2,1,0:T(8,128)S(1)} %get-tuple-element.25), channel_id=1, source_target_pairs={{0,2},{1,3},{2,0},{3,1},{4,6},{5,7},{6,4},{7,5},{8,10},{9,11},{10,... | collective-permute-start | bytes 393224 | tf_op jit(solution)/shard_map/ppermute | solution.py:321
  18.0 7.2 %collective-permute-start.7 = (f32[4,16,512]{2,1,0:T(8,128)S(1)}, f32[4,16,512]{2,1,0:T(8,128)S(1)}, u32[]{:S(2)}, u32[]{:S(2)}) collective-permute-start(f32[4,16,512]{2,1,0:T(8,128)S(1)} %get-tuple-element.26), channel_id=1, source_target_pairs={{0,3},{1,0},{2,1},{3,2},{4,7},{5,4},{6,5},{7,6},{8,11},{9,8},{10,9... | collective-permute-start | bytes 393224 | tf_op jit(solution)/shard_map/ppermute | solution.py:321
